TPU v7x, 128 devices: a whole 4x4x4 slice. The times are simulated.
128 devices in a mesh: group: 4 (over z), shard: 32 (over x, y, core).
Axes of the slice: x: 4, y: 4, z: 4, core: 2. Of those that a mesh axis runs over, the one named last changes fastest.
Arguments:
- embeddings: bfloat16 [49152, 768], P(('group', 'shard')), may hold values from -0.21875 to 0.21875
- members: int32 [49152], P(('group', 'shard')), may hold values from 0 to 8191, as said below
- counts: int32 [4, 32], replicated, may hold values from 96 to 384
Outputs:
- row_potential: float32 [49152], P(('group', 'shard'))
- col_potential: float32 [49152], P(('group', 'shard'))
- coarse_potential: float32 [8192], P(('group', 'shard'))
Inputs may be any that keep to these rules, and one draw needn't show every extreme that they name: `members`: tracklets of shard index s (block b with b % 32 = s) name prototypes (k // (256 // 4)) * 32 * (256 // 4) + s * (256 // 4) + k % (256 // 4) for k below 256; every prototype is named by a tracklet at row r < 256 // 4 of some block.
All inputs are finite; a program needn't handle non-finite values.
Results may differ from a plain program's by a relative error of at most 0.0065.
Values may be sent and summed in bfloat16 or wider, within the bound.
No kernel may reach another device: no remote copies, remote signals or barrier semaphores. Data moves between devices by JAX's collectives and lax.ppermute only.
A program may use at most 128 MiB of HBM per device.

v0:
```python
import jax
import jax.numpy as jnp
from jax import lax
from jax.sharding import PartitionSpec as P

PROTO_BLOCK = 256
FINE_PRE = 2
COARSE = 2


EPS = 0.01
BIG = 1e30


def local(embeddings, members, counts):
    rows = embeddings.shape[0]
    nshard = lax.axis_size("shard")
    ngroup = lax.axis_size("group")
    group_idx = lax.axis_index("group")
    shard_idx = lax.axis_index("shard")
    group_rows = rows * nshard
    quarter = PROTO_BLOCK // ngroup
    group_counts = lax.dynamic_index_in_dim(counts, group_idx, 0, keepdims=False)
    my_count = lax.dynamic_index_in_dim(group_counts, shard_idx, 0, keepdims=False)
    col_valid = jnp.arange(group_rows) % rows < jnp.repeat(
        group_counts, rows, total_repeat_length=group_rows
    )
    row_valid = jnp.arange(rows) < my_count
    log_mass = -jnp.log(jnp.sum(group_counts).astype(jnp.float32))
    my_start = shard_idx * rows
    row_ids = my_start + jnp.arange(rows)
    piece = lax.all_gather(embeddings, "shard", axis=0, tiled=True)
    width = piece.shape[0]
    block = 1.0 - lax.dot_general(
        embeddings, piece, (((1,), (1,)), ((), ())), preferred_element_type=jnp.float32
    )
    cols = jnp.arange(width)
    live = lax.slice_in_dim(col_valid, 0, width, axis=0)
    keep = live[None, :] & (cols[None, :] != row_ids[:, None])
    cost = jnp.where(keep, block, BIG)

    def update_rows(h_all):
        scores = (h_all[None, :] - cost) / EPS
        top = jnp.max(scores, axis=1)
        total = jnp.sum(jnp.exp(scores - top[:, None]), axis=1)
        out = EPS * log_mass - EPS * (top + jnp.log(total))
        return jnp.where(row_valid, out, 0.0)

    def pull(h_loc):
        return lax.all_gather(h_loc, "shard", axis=0, tiled=True)

    def column_update(f_loc):
        return update_rows(pull(f_loc))

    col_loc = jnp.zeros((rows,), jnp.float32)
    row_loc = col_loc
    for step in range(FINE_PRE):
        if step == 0:
            col_all = jnp.zeros((group_rows,), jnp.float32)
        else:
            col_all = pull(col_loc)
        row_loc = update_rows(col_all)
        col_loc = column_update(row_loc)
    local_ids = members // (nshard * quarter) * quarter + members % quarter
    onehot = (local_ids[:, None] == jnp.arange(PROTO_BLOCK)[None, :]) & row_valid[:, None]
    onehot_bf = onehot.astype(jnp.bfloat16)
    sums = lax.dot_general(
        onehot_bf, embeddings, (((0,), (0,)), ((), ())), preferred_element_type=jnp.float32
    )
    sizes = jnp.sum(onehot.astype(jnp.float32), axis=0)
    pooled_sums, pooled_sizes = (
        lax.psum_scatter(sums, "group", scatter_dimension=0, tiled=True),
        lax.psum_scatter(sizes, "group", scatter_dimension=0, tiled=True),
    )
    total_valid = jnp.sum(counts).astype(jnp.float32)
    means = (pooled_sums / pooled_sizes[:, None]).astype(jnp.bfloat16)
    plog = jnp.log(pooled_sizes / total_valid)
    my_protos = (group_idx * nshard + shard_idx) * quarter + jnp.arange(quarter)
    piece = lax.all_gather(means, ("group", "shard"), axis=0, tiled=True)
    width = piece.shape[0]
    block = 1.0 - lax.dot_general(
        means, piece, (((1,), (1,)), ((), ())), preferred_element_type=jnp.float32
    )
    cols = jnp.arange(width)
    kcost = jnp.where(cols[None, :] != my_protos[:, None], block, BIG)

    def coarse_update(h_all):
        scores = (h_all[None, :] - kcost) / EPS
        top = jnp.max(scores, axis=1)
        total = jnp.sum(jnp.exp(scores - top[:, None]), axis=1)
        return EPS * plog - EPS * (top + jnp.log(total))

    def coarse_pull(h_loc):
        return lax.all_gather(h_loc, ("group", "shard"), axis=0, tiled=True)

    coarse_loc = jnp.zeros((quarter,), jnp.float32)
    for step in range(COARSE):
        if step == 0:
            coarse_all = jnp.zeros((kcost.shape[1],), jnp.float32)
        else:
            coarse_all = coarse_pull(coarse_loc)
        upper = coarse_update(coarse_all)
        coarse_loc = coarse_update(coarse_pull(upper))
    block_vals = lax.all_gather(coarse_loc, "group", axis=0, tiled=True)
    boost = jnp.dot(onehot.astype(jnp.float32), block_vals, precision=lax.Precision.HIGHEST)
    row_loc = row_loc + boost
    col_loc = column_update(row_loc)
    row_loc = update_rows(pull(col_loc))
    return (row_loc, col_loc, coarse_loc)


def solution(mesh):
    placed = (P(("group", "shard"), None), P(("group", "shard")), P())
    return jax.shard_map(
        local,
        mesh=mesh,
        in_specs=placed,
        out_specs=(P(("group", "shard")), P(("group", "shard")), P(("group", "shard"))),
        check_vma=False,
    )
```

profile of v0, /device:TPU:0, one launch (start us, length us, event | category | flops | bytes accessed | tf_op | source)
XLA Modules:
  0.0 536.3 jit_solution(11500123067215914438)
XLA Ops:
  7.2 1.3 dynamic_slice.8
  8.5 0.6 iota_compare_fusion.3
  9.1 0.7 fusion.25
  9.8 2.5 fusion.13
  12.4 1.3 fusion.30
  14.6 11.9 %all-reduce.4 = f32[256]{0:T(256)S(1)} all-reduce(f32[256]{0:T(256)S(1)} %convert_reduce_fusion), channel_id=2, replica_groups=mesh['group'=4,'shard'=32] {'group'}, use_global_device_ids=true, to_apply=%region_8.9.clone | all-reduce | flops 256 | bytes 2048
  26.5 11.1 %reduce-scatter.2.cloned.1.call-done = f32[64,768]{1,0:T(8,128)} async-done(((f32[256,768]{1,0:T(8,128)}), f32[64,768]{1,0:T(8,128)}) %reduce-scatter.2.cloned.1.call-update) | async-done | bytes 196624 | tf_op jit(solution)/shard_map/reduce_scatter | solution.py:72
  37.6 1.6 divide_convert_fusion
  39.3 0.7 all-gather.7.cloned.1.call-update
  40.0 1.3 reduce_sum.113
  41.3 1.3 fusion.28
  44.7 0.7 fusion.32
  45.4 0.7 fusion.31
  46.1 21.8 %fusion.19 = pred[12288]{0:T(1024)(128)(4,1)S(1)} fusion(pred[12288]{0:T(1024)(128)(4,1)} %constant.235, pred[12288]{0:T(1024)(128)(4,1)} %constant.236, pred[12288]{0:T(1024)(128)(4,1)} %constant.237, pred[12288]{0:T(1024)(128)(4,1)} %constant.238, pred[12288]{0:T(1024)(128)(4,1)} %constant.239, pred[12288]{0:T(1024)(128)(4,1)} %constant.240, ...), kind=kLoop, calls=%fused_computation.44 | loop fusion | flops 466944 | bytes 393344 | tf_op jit(solution)/shard_map/lt | solution.py:25
  67.9 45.7 %all-gather.9.cloned.1.call-done = bf16[8192,768]{1,0:T(8,128)(2,1)} async-done(((bf16[64,768]{1,0:T(8,128)(2,1)}), bf16[8192,768]{1,0:T(8,128)(2,1)}) %all-gather.9.cloned.1.call-update) | async-done | bytes 12582928 | tf_op jit(solution)/shard_map/all_gather | solution.py:79
  113.7 8.7 %fusion.7 = (f32[64]{0:T(128)S(1)}, f32[64,8192]{1,0:T(8,128)S(1)}) fusion(bf16[64,768]{1,0:T(8,128)(2,1)} %divide_convert_fusion, bf16[8192,768]{1,0:T(8,128)(2,1)} %all-gather.9.cloned.1.call-done, s32[64]{0:T(128)S(1)} %iota_add_fusion.1), kind=kOutput, calls=%fused_computation.29 | convolution fusion | flops 808452032 | bytes 14778880 | tf_op jit(solution)/shard_map/dot_general | solution.py:81
  122.3 0.6 exponential_reduce_fusion.8
  123.1 67.0 %all-reduce = f32[8192]{0:T(1024)S(1)} all-reduce(f32[8192]{0:T(1024)S(1)} %subtract_dynamic-update-slice_fusion.2), channel_id=1, replica_groups=mesh['group'=4,'shard'=32] {'group','shard'}, use_global_device_ids=true, to_apply=%add | all-reduce | flops 8192 | bytes 65536
  190.1 0.3 fusion.8
  190.5 0.6 exponential_reduce_fusion.7
  191.2 64.0 %all-reduce.1 = f32[8192]{0:T(1024)S(1)} all-reduce(f32[8192]{0:T(1024)S(1)} %subtract_dynamic-update-slice_fusion.1), channel_id=1, replica_groups=mesh['group'=4,'shard'=32] {'group','shard'}, use_global_device_ids=true, to_apply=%add.1 | all-reduce | flops 8192 | bytes 65536
  255.2 0.3 fusion.9
  255.5 0.6 exponential_reduce_fusion.6
  256.3 62.2 %all-reduce.2 = f32[8192]{0:T(1024)S(1)} all-reduce(f32[8192]{0:T(1024)S(1)} %subtract_dynamic-update-slice_fusion), channel_id=1, replica_groups=mesh['group'=4,'shard'=32] {'group','shard'}, use_global_device_ids=true, to_apply=%add.2 | all-reduce | flops 8192 | bytes 65536
  318.5 0.3 fusion.10
  318.8 0.6 exponential_reduce_fusion.5
  319.4 0.6 fusion.29
  320.0 10.7 %all-reduce.3 = f32[256]{0:T(256)S(1)} all-reduce(f32[256]{0:T(256)S(1)} %get-tuple-element.17), channel_id=1, replica_groups=mesh['group'=4,'shard'=32] {'group'}, use_global_device_ids=true, to_apply=%add.3 | all-reduce | flops 256 | bytes 2048
  330.7 0.4 convolution_reduce_fusion
  331.2 16.4 %fusion.1 = (f32[384]{0:T(512)S(1)}, f32[384,12288]{1,0:T(8,128)}) fusion(bf16[384,768]{1,0:T(8,128)(2,1)S(1)} %copy-done, bf16[12288,768]{1,0:T(8,128)(2,1)} %all-gather.7.cloned.1.call-done, s32[384]{0:T(512)S(1)} %iota_add_fusion, pred[12288]{0:T(1024)(128)(4,1)S(1)} %fusion.19), kind=kOutput, calls=%fused_computation.13 | convolution fusion | flops 7280786944 | bytes 38353920 | tf_op jit(solution)/shard_map/dot_general | solution.py:34
  347.6 10.1 %exponential_reduce_fusion.4 = f32[384]{0:T(512)S(1)} fusion(f32[384,12288]{1,0:T(8,128)} %get-tuple-element.56, f32[384]{0:T(512)S(1)} %get-tuple-element.55), kind=kLoop, calls=%fused_computation.8 | loop fusion | flops 18873984 | bytes 18877440 | tf_op jit(solution)/shard_map/reduce_sum | solution.py:45
  357.8 0.6 subtract_select_fusion.4
  358.4 21.7 %all-gather = f32[32,1,384]{2,1,0:T(1,128)S(1)} all-gather(f32[1,1,384]{2,1,0:T(1,128)S(1)} %reshape.250), channel_id=1, replica_groups=mesh['group'=4,'shard'=32] {'shard'}, dimensions={0}, use_global_device_ids=true | all-gather | bytes 50688 | tf_op jit(solution)/shard_map/all_gather | solution.py:50
  380.2 8.7 %fusion.2 = f32[384]{0:T(512)S(1)} fusion(f32[384,12288]{1,0:T(8,128)} %get-tuple-element.56, f32[12288]{0:T(1024)S(1)} %bitcast.48), kind=kLoop, calls=%fused_computation.14 | loop fusion | flops 14155392 | bytes 18925056 | tf_op jit(solution)/shard_map/reduce_max | solution.py:44
  388.9 10.5 %exponential_reduce_fusion.3 = f32[384]{0:T(512)S(1)} fusion(f32[384,12288]{1,0:T(8,128)} %get-tuple-element.56, f32[384]{0:T(512)S(1)} %fusion.2, f32[12288]{0:T(1024)S(1)} %bitcast.49), kind=kLoop, calls=%fused_computation.6 | loop fusion | flops 18873984 | bytes 18926592 | tf_op jit(solution)/shard_map/reduce_sum | solution.py:45
  399.3 0.6 subtract_select_fusion.3
  400.0 24.4 %all-gather.1 = f32[32,1,384]{2,1,0:T(1,128)S(1)} all-gather(f32[1,1,384]{2,1,0:T(1,128)S(1)} %reshape.252), channel_id=1, replica_groups=mesh['group'=4,'shard'=32] {'shard'}, dimensions={0}, use_global_device_ids=true | all-gather | bytes 50688 | tf_op jit(solution)/shard_map/all_gather | solution.py:50
  424.4 8.7 %fusion.3 = f32[384]{0:T(512)S(1)} fusion(f32[384,12288]{1,0:T(8,128)} %get-tuple-element.56, f32[12288]{0:T(1024)S(1)} %bitcast.50), kind=kLoop, calls=%fused_computation.15 | loop fusion | flops 14155392 | bytes 18925056 | tf_op jit(solution)/shard_map/reduce_max | solution.py:44
  433.1 10.5 %exponential_reduce_fusion.2 = f32[384]{0:T(512)S(1)} fusion(f32[384,12288]{1,0:T(8,128)} %get-tuple-element.56, f32[384]{0:T(512)S(1)} %fusion.3, f32[12288]{0:T(1024)S(1)} %bitcast.51), kind=kLoop, calls=%fused_computation.4 | loop fusion | flops 18873984 | bytes 18926592 | tf_op jit(solution)/shard_map/reduce_sum | solution.py:45
  443.5 0.6 select_add_fusion
  444.2 21.7 %all-gather.2 = f32[32,1,384]{2,1,0:T(1,128)S(1)} all-gather(f32[1,1,384]{2,1,0:T(1,128)S(1)} %reshape.254), channel_id=1, replica_groups=mesh['group'=4,'shard'=32] {'shard'}, dimensions={0}, use_global_device_ids=true | all-gather | bytes 50688 | tf_op jit(solution)/shard_map/all_gather | solution.py:50
  465.8 8.4 %fusion.4 = f32[384]{0:T(512)S(1)} fusion(f32[384,12288]{1,0:T(8,128)} %get-tuple-element.56, f32[12288]{0:T(1024)S(1)} %bitcast.52), kind=kLoop, calls=%fused_computation.16 | loop fusion | flops 14155392 | bytes 18925056 | tf_op jit(solution)/shard_map/reduce_max | solution.py:44
  474.2 10.2 %exponential_reduce_fusion.1 = f32[384]{0:T(512)S(1)} fusion(f32[384,12288]{1,0:T(8,128)} %get-tuple-element.56, f32[384]{0:T(512)S(1)} %fusion.4, f32[12288]{0:T(1024)S(1)} %bitcast.53), kind=kLoop, calls=%fused_computation.2 | loop fusion | flops 18873984 | bytes 18926592 | tf_op jit(solution)/shard_map/reduce_sum | solution.py:45
  484.4 0.6 subtract_select_fusion.2
  485.0 24.2 %all-gather.3 = f32[32,1,384]{2,1,0:T(1,128)S(1)} all-gather(f32[1,1,384]{2,1,0:T(1,128)S(1)} %reshape.256), channel_id=1, replica_groups=mesh['group'=4,'shard'=32] {'shard'}, dimensions={0}, use_global_device_ids=true | all-gather | bytes 50688 | tf_op jit(solution)/shard_map/all_gather | solution.py:50
  509.2 8.7 %fusion.5 = f32[384]{0:T(512)S(1)} fusion(f32[384,12288]{1,0:T(8,128)} %get-tuple-element.56, f32[12288]{0:T(1024)S(1)} %bitcast.46), kind=kLoop, calls=%fused_computation.17 | loop fusion | flops 14155392 | bytes 18925056 | tf_op jit(solution)/shard_map/reduce_max | solution.py:44
  517.9 10.4 %exponential_reduce_fusion = f32[384]{0:T(512)S(1)} fusion(f32[384,12288]{1,0:T(8,128)} %get-tuple-element.56, f32[384]{0:T(512)S(1)} %fusion.5, f32[12288]{0:T(1024)S(1)} %bitcast.47), kind=kLoop, calls=%fused_computation | loop fusion | flops 18873984 | bytes 18926592 | tf_op jit(solution)/shard_map/reduce_sum | solution.py:45
  528.3 1.2 subtract_select_fusion.1
  (25 shorter events, 1.1 us)
Async XLA Ops:
  7.2 30.4 %reduce-scatter.2.cloned.1.call-start = ((), (), s32[]{:S(2)}) async-start(), calls=%async_computation.2 | async-start | bytes 983040 | tf_op jit(solution)/shard_map/reduce_scatter | solution.py:72
  12.3 101.3 %all-gather.9.cloned.1.call-start = ((), (), s32[]{:S(2)}) async-start(), calls=%async_computation.3 | async-start | bytes 12681216 | tf_op jit(solution)/shard_map/all_gather | solution.py:79
  39.3 291.9 %all-gather.7.cloned.1.call-start = ((), (), s32[]{:S(2)}) async-start(), calls=%async_computation.1 | async-start | bytes 19464192 | tf_op jit(solution)/shard_map/all_gather | solution.py:32
  67.9 263.2 %copy-start = (bf16[384,768]{1,0:T(8,128)(2,1)S(1)}, bf16[384,768]{1,0:T(8,128)(2,1)}, u32[]{:S(2)}) copy-start(bf16[384,768]{1,0:T(8,128)(2,1)} %param.5) | copy-start | bytes 1769476
  485.0 43.3 %copy-start.1 = (f32[384]{0:T(512)}, f32[384]{0:T(512)S(1)}, u32[]{:S(2)}) copy-start(f32[384]{0:T(512)S(1)} %subtract_select_fusion.2) | copy-start | bytes 4612
Sparse Core Ops, SparseCore 0:
  12.5 25.1 reduce-scatter.1
  40.7 72.9 all-gather.8
  115.9 78.3 all-gather.6
where the time goes:
time: 547 us; the launch traced here: 536 us
  blocking collectives  308 us (56%)
  other arithmetic  122 us (22%)
  waiting for transfers between devices  57.6 us (11%)
  matrix products  28 us (5%)
  between operations  16.8 us (3%)
    unnamed x5, blocking collectives  216 us
    all_gather x4, blocking collectives, pull(): return lax.all_gather(h_loc, 'shard', axis=0, tiled=True)  92 us
    reduce_sum x5, other arithmetic, update_rows(): total = jnp.sum(jnp.exp(scores - top[:, None]), axis=1)  51.7 us
    all_gather x1, waiting for transfers between devices, local(): piece = lax.all_gather(means, ('group', 'shard'), axis=0, tiled=True)  45.7 us
    reduce_max x4, other arithmetic, update_rows(): top = jnp.max(scores, axis=1)  34.5 us
    lt x1, other arithmetic, local(): jnp.arange(group_rows) % rows  21.8 us
    dot_general x1, matrix products, local(): lax.dot_general(embeddings, piece, (((1,), (1,)), ((), ())), preferred_el...  16.4 us
    reduce_scatter x1, waiting for transfers between devices, local(): lax.psum_scatter(sums, 'group', scatter_dimension=0, tiled=True)  11.1 us
  transfers between devices with their start and end apart: 3, of which 2 were waited for; matrix products, arithmetic and copies ran while one was open for 8% of the time, Pallas kernels for 0%

commit v1 on v0

v1 whole, which is shorter than its diff:
```python
import math

import jax
import jax.numpy as jnp
from jax import lax
from jax.experimental import pallas as pl
from jax.experimental.pallas import tpu as pltpu
from jax.sharding import Mesh, PartitionSpec as P


PROTO_BLOCK = 256
EPS = 0.01
SC = math.log2(math.e) / EPS
NEG = -1e30
LOW, HIGH = 2.0 ** -64, 2.0 ** 120
F32 = jnp.float32
BF16 = jnp.bfloat16
MIB = 2 ** 20
X, Y, Z = 4, 4, 4
PAD = 128

VMEM = pl.BlockSpec(memory_space=pltpu.VMEM)
SMEM = pl.BlockSpec(memory_space=pltpu.SMEM)
ANY = pl.BlockSpec(memory_space=pl.ANY)


def call(body, out_shape, in_specs, scratch=(), limit=24, name=None, flops=0, nbytes=0):
    return pl.pallas_call(
        body,
        out_shape=out_shape,
        in_specs=in_specs,
        out_specs=jax.tree.map(lambda _: VMEM, out_shape),
        scratch_shapes=list(scratch),
        compiler_params=pltpu.CompilerParams(vmem_limit_bytes=limit * MIB),
        cost_estimate=pl.CostEstimate(flops=flops, bytes_accessed=nbytes, transcendentals=0),
        name=name,
    )


def sds(shape, dtype=F32):
    return jax.ShapeDtypeStruct(shape, dtype)


def iota(shape, dim):
    return lax.broadcasted_iota(jnp.int32, shape, dim)


def to_lanes(col):
    n = col.shape[0]
    eye = iota((128, 128), 0) == iota((128, 128), 1)
    return jnp.concatenate(
        [
            jnp.sum(jnp.where(eye, col[k * 128:(k + 1) * 128], 0.0), axis=0, keepdims=True)
            for k in range(n // 128)
        ],
        axis=0,
    )


def to_rows(vals, out_ref):
    for k in range(vals.shape[0]):
        out_ref[k * 128:(k + 1) * 128, :] = jnp.transpose(
            jnp.broadcast_to(vals[k:k + 1, :], (128, 128))
        )


def lse2(parts):
    top = parts[0]
    for p in parts[1:]:
        top = jnp.maximum(top, p)
    total = jnp.exp2(parts[0] - top)
    for p in parts[1:]:
        total = total + jnp.exp2(p - top)
    return top + jnp.log2(total)


def in_range(total):
    return jnp.sum(jnp.where((total > LOW) & (total < HIGH), 0.0, 1.0)) == 0.0


def reduce_columns(tile, h, out_ref, wide_ref):
    rows, cols = tile.shape
    shift = jnp.max(h)
    lane, sub = iota((8, 128), 1), iota((8, 128), 0)

    def spread(by):
        for k in range(cols // 128):
            wide_ref[:, k * 128:(k + 1) * 128] = jnp.broadcast_to(h[k:k + 1, :] - by, (8, 128))

    spread(shift)

    def fast(r, _):
        acc = jnp.zeros((8, 128), F32)
        for g in range(16):
            s = tile[pl.ds(pl.multiple_of(r * 128 + g * 8, 8), 8), :] + wide_ref[...]
            part = jnp.sum(jnp.exp2(s), axis=1, keepdims=True)
            acc = acc + jnp.where(lane == sub + 8 * g, part, 0.0)
        out_ref[pl.ds(r, 1), :] = jnp.sum(acc, axis=0, keepdims=True)
        return 0

    lax.fori_loop(0, rows // 128, fast, 0, unroll=2)
    total = out_ref[0:rows // 128, :]
    good = in_range(total)

    @pl.when(good)
    def _():
        out_ref[0:rows // 128, :] = jnp.log2(total) + shift

    @pl.when(jnp.logical_not(good))
    def _():
        spread(0.0)

        def safe(r, _):
            acc = jnp.zeros((8, 128), F32)
            for g in range(16):
                s = tile[pl.ds(pl.multiple_of(r * 128 + g * 8, 8), 8), :] + wide_ref[...]
                top = jnp.max(s, axis=1, keepdims=True)
                part = top + jnp.log2(jnp.sum(jnp.exp2(s - top), axis=1, keepdims=True))
                acc = acc + jnp.where(lane == sub + 8 * g, part, 0.0)
            out_ref[pl.ds(r, 1), :] = jnp.sum(acc, axis=0, keepdims=True)
            return 0

        lax.fori_loop(0, rows // 128, safe, 0)


def safe_rows(tile, tall_ref, out_ref):
    rows, cols = tile.shape
    width, chunk = 128, 128
    for strip in range(cols // width):
        at = pl.ds(strip * width, width)

        def safe(c, carry):
            top, total = carry
            part = pl.ds(pl.multiple_of(c * chunk, chunk), chunk)
            s = (tile[part, at] + tall_ref[part, :]).reshape(chunk // 8, 8, width)
            now = jnp.maximum(top, jnp.max(s, axis=0))
            return now, total * jnp.exp2(top - now) + jnp.sum(jnp.exp2(s - now[None]), axis=0)

        top, total = lax.fori_loop(
            0, rows // chunk, safe, (jnp.full((8, width), NEG, F32), jnp.zeros((8, width), F32))
        )
        best = jnp.max(top, axis=0, keepdims=True)
        total = jnp.sum(total * jnp.exp2(top - best), axis=0, keepdims=True)
        out_ref[strip:strip + 1, :] = best + jnp.log2(total)


def reduce_rows(tile, h, out_ref, tall_ref):
    rows, cols = tile.shape
    shift = jnp.max(h)
    to_rows(h - shift, tall_ref)
    width = 256
    chunk = 64
    groups = width // 128
    for strip in range(cols // width):
        at = pl.ds(strip * width, width)

        def fast(c, acc):
            part = pl.ds(pl.multiple_of(c * chunk, chunk), chunk)
            add = tall_ref[part, :]
            s = tile[part, at] + jnp.concatenate([add] * groups, axis=1)
            return acc + jnp.sum(jnp.exp2(s).reshape(chunk // 8, 8, width), axis=0)

        acc = lax.fori_loop(0, rows // chunk, fast, jnp.zeros((8, width), F32), unroll=2)
        acc = jnp.sum(acc, axis=0, keepdims=True)
        for k in range(groups):
            row = strip * groups + k
            out_ref[row:row + 1, :] = acc[:, k * 128:(k + 1) * 128]
    total = out_ref[0:cols // 128, :]
    good = in_range(total)

    @pl.when(good)
    def _():
        out_ref[0:cols // 128, :] = jnp.log2(total) + shift

    @pl.when(jnp.logical_not(good))
    def _():
        to_rows(h, tall_ref)
        safe_rows(tile, tall_ref, out_ref)


def place(idx):
    return idx[0], idx[1], idx[2], idx[3]


def count_at(counts, z, x, y, c):
    return counts[z, (x * Y + y) * 2 + c]


def row_counts(counts, idx):
    z, x, y, c = place(idx)
    return [count_at(counts, z, x, lax.rem(y + dy, Y), lax.rem(c + dc, 2)) for dc in range(2) for dy in range(Y)]


def col_counts(counts, idx):
    z, x, y, c = place(idx)
    return [count_at(counts, z, lax.rem(x + dx, X), y, c) for dx in range(X)]


def group_total(counts, idx):
    n = counts[idx[0], 0]
    for s in range(1, X * Y * 2):
        n = n + counts[idx[0], s]
    return n


def live_mask(shape, block_counts, per):
    at = iota((per, 128), 0) * 128 + iota((per, 128), 1)
    return jnp.concatenate([jnp.where(at < n, 1.0, 0.0) for n in block_counts], axis=0) > 0.0


def log2_of(n):
    return jnp.log2(jnp.full((1, 128), n, jnp.int32).astype(F32))


def from_columns(parts, first, per):
    blocks = []
    for dx in range(X):
        blocks.append(
            lse2([p[first + (dx + k) % X * per:first + (dx + k) % X * per + per, :] for k, p in enumerate(parts)])
        )
    return jnp.concatenate(blocks, axis=0)


def gather_columns(parts, first, per):
    return jnp.concatenate([parts[(X - dx) % X][first:first + per, :] for dx in range(X)], axis=0)


def fold_y(parts, first, per):
    blocks = []
    for dc in range(2):
        for dy in range(Y):
            rows = [first + (dc * Y + (dy + k) % Y) * per for k in range(Y)]
            blocks.append(lse2([p[r:r + per, :] for p, r in zip(parts, rows)]))
    return jnp.concatenate(blocks, axis=0)


def fold_core(mine, other, first, per):
    half = Y * per
    return jnp.concatenate(
        [
            lse2([mine[first:first + half, :], other[first + half:first + 2 * half, :]]),
            lse2([mine[first + half:first + 2 * half, :], other[first:first + half, :]]),
        ],
        axis=0,
    )


def pool_kernel(counts, idx, emb, members, own, far1, far2, far3):
    z, x, y, c = place(idx)
    quarter = PROTO_BLOCK // Z
    ids = members[...]
    turn = lax.rem(lax.shift_right_logical(ids, 11) - z + Z, Z)
    local = turn * quarter + jnp.bitwise_and(ids, quarter - 1)
    rows = emb.shape[0]
    live = iota((1, rows), 1) < count_at(counts, z, x, y, c)
    hot = ((iota((PROTO_BLOCK, rows), 0) == local) & live).astype(BF16)
    sums = jnp.dot(hot, emb[...], preferred_element_type=F32)
    sizes = jnp.dot(hot, jnp.ones((rows, PAD), BF16), preferred_element_type=F32)
    d = emb.shape[1]
    own[:, 0:d] = sums[0:quarter]
    own[:, d:] = sizes[0:quarter]
    coded = code_sizes(sizes)
    for k, ref in ((1, far1), (2, far2), (3, far3)):
        ref[:, 0:d] = sums[k * quarter:(k + 1) * quarter].astype(BF16)
        ref[:, d:] = coded[k * quarter:(k + 1) * quarter]


def code_sizes(sizes):
    high = jnp.floor(sizes * (1.0 / 256.0))
    low = sizes - 256.0 * high
    return jnp.where(iota(sizes.shape, 1) < 64, high, low).astype(BF16)


def read_sizes(block, d):
    coded = block[:, d:].astype(F32)
    return coded[:, 0:1] * 256.0 + coded[:, 64:65]


def means_kernel(own, far1, far2, far3, out):
    d = own.shape[1] - PAD
    sums = own[:, 0:d]
    sizes = own[:, d:d + 1]
    for ref in (far1, far2, far3):
        block = ref[...]
        sums = sums + block[:, 0:d].astype(F32)
        sizes = sizes + read_sizes(block, d)
    out[:, 0:d] = (sums / sizes).astype(BF16)
    out[:, d:] = code_sizes(jnp.broadcast_to(sizes, (sizes.shape[0], PAD)))


def join_kernel(counts, own, far1, far2, far3, means, plog):
    d = own.shape[1] - PAD
    quarter = own.shape[0]
    total = counts[0, 0]
    for z in range(Z):
        for s in range(X * Y * 2):
            if z + s > 0:
                total = total + counts[z, s]
    sizes = []
    for k, ref in enumerate((own, far1, far2, far3)):
        block = ref[...]
        means[k * quarter:(k + 1) * quarter, :] = block[:, 0:d]
        sizes.append(jnp.broadcast_to(read_sizes(block, d), (quarter, 128)))
    plog[...] = jnp.zeros(plog.shape, F32)
    plog[0:2, :] = jnp.log2(to_lanes(jnp.concatenate(sizes, axis=0))) - log2_of(total)


def fetch(pieces, buf, sems):
    size = sum(p.shape[0] for p in pieces[0])
    for b, parts in enumerate(pieces):
        at = b * size
        for p in parts:
            n = p.shape[0]
            pltpu.make_async_copy(p, buf.at[pl.ds(at, n)], sems.at[b]).start()
            at += n

    def wait(b):
        into = buf.at[pl.ds(b * size, size)]
        pltpu.make_async_copy(into, into, sems.at[b]).wait()

    return wait


def tile_of(own, xs, ys, rows_buf, cols_buf, row_sems, col_sems):
    xa, xb, xc, xd = xs
    ya, yb, yc, yd, so, sa, sb, sc, sd = ys
    wait_cols = fetch([[own], [xb], [xc, xd], [xa]], cols_buf, col_sems)
    wait_rows = fetch([[own], [yb], [yc, yd], [ya], [so], [sb], [sc, sd], [sa]], rows_buf, row_sems)
    for b in range(X):
        wait_cols(b)
    for b in range(2 * Y):
        wait_rows(b)


def dot_t(a, b):
    return lax.dot_general(a, b, (((1,), (1,)), ((), ())), preferred_element_type=F32) * SC


def coarse_tile_kernel(own, *refs):
    xs, ys = refs[0:4], refs[4:13]
    plog, tile, payload, rows_buf, cols_buf, row_sems, col_sems, wide = refs[13:]
    tile_of(own, xs, ys, rows_buf, cols_buf, row_sems, col_sems)
    rows, cols = tile.shape
    step = 256

    def body(i, _):
        at = pl.ds(pl.multiple_of(i * step, step), step)
        tile[at, :] = dot_t(rows_buf[at, :], cols_buf[...])
        return 0

    lax.fori_loop(0, rows // step, body, 0)
    n = own.shape[0]
    eye = iota((n, n), 0) == iota((n, n), 1)
    tile[0:n, 0:n] = jnp.where(eye, NEG, tile[0:n, 0:n])
    payload[...] = jnp.zeros(payload.shape, F32)
    reduce_columns(tile, jnp.zeros((cols // 128, 128), F32), payload, wide)
    payload[rows // 128:rows // 128 + 2, :] = plog[0:2, :]


def fine_tile_kernel(counts, idx, own, *refs):
    xs, ys = refs[0:4], refs[4:13]
    tile, part, rows_buf, cols_buf, row_sems, col_sems, tall, acc = refs[13:]
    n = own.shape[0]
    for b, count in enumerate(row_counts(counts, idx)):
        tall[b * n:(b + 1) * n, :] = jnp.where(iota((n, 128), 0) < count, 0.0, NEG)
    tile_of(own, xs, ys, rows_buf, cols_buf, row_sems, col_sems)
    rows, cols = tile.shape
    step, wide = 256, 512
    acc[...] = jnp.zeros(acc.shape, F32)

    def body(i, _):
        at = pl.ds(pl.multiple_of(i * step, step), step)
        for j in range(cols // wide):
            across = pl.ds(j * wide, wide)
            s = dot_t(rows_buf[at, :], cols_buf[across, :])
            same = iota((step, wide), 0) + i * step == iota((step, wide), 1) + j * wide
            if j * wide < n:
                s = jnp.where(same & (iota((step, wide), 1) + j * wide < n), NEG, s)
            tile[at, across] = s
            s = s + jnp.concatenate([tall[at, :]] * (wide // 128), axis=1)
            acc[:, across] += jnp.sum(jnp.exp2(s).reshape(step // 8, 8, wide), axis=0)
        return 0

    lax.fori_loop(0, rows // step, body, 0)
    total = jnp.sum(acc[...], axis=0, keepdims=True)
    for k in range(cols // 128):
        part[k:k + 1, :] = total[:, k * 128:(k + 1) * 128]
    total = part[0:cols // 128, :]
    good = in_range(total)

    @pl.when(good)
    def _():
        part[0:cols // 128, :] = jnp.log2(total)

    @pl.when(jnp.logical_not(good))
    def _():
        safe_rows(tile, tall, part)


def fold_y_kernel(plan, *refs):
    parts, out = refs[0:Y], refs[Y]
    out[...] = jnp.zeros(out.shape, F32)
    for first, per in plan["lse"]:
        n = 2 * Y * per
        out[first:first + n, :] = fold_y(parts, first, per)
    if plan["plog"] is not None:
        first, into = plan["plog"]
        out[into:into + 2 * Y, :] = jnp.concatenate(
            [parts[(Y - dy) % Y][first:first + 2, :] for dy in range(Y)], axis=0
        )


def coarse2_kernel(mine, other, part, plog, members, tile, payload, plog_rows, tall):
    plog_rows[0:8, :] = mine[16:24, :]
    plog_rows[8:16, :] = other[16:24, :]
    h = plog_rows[...] + SC - fold_core(mine, other, 0, 2)
    payload[...] = jnp.zeros(payload.shape, F32)
    reduce_rows(tile, h, payload, tall)
    payload[8:20, :] = part[...]
    payload[20:22, :] = plog[0:2, :]
    payload[22:25, :] = members[...].astype(F32)


def fine_h(lse, counts, idx, block_counts, per):
    live = live_mask(lse.shape, block_counts, per)
    return live, SC - log2_of(group_total(counts, idx)) - lse


def step3_kernel(counts, idx, p0, p1, p2, p3, ktile, tile, payload, plog_cols, members, wide, kwide):
    parts = (p0, p1, p2, p3)
    plog_cols[...] = gather_columns(parts, 20, 2)
    members[...] = gather_columns(parts, 22, 3)
    payload[...] = jnp.zeros(payload.shape, F32)
    live, h = fine_h(from_columns(parts, 8, 3), counts, idx, col_counts(counts, idx), 3)
    reduce_columns(tile, jnp.where(live, h, NEG), payload.at[16:40, :], wide)
    h = plog_cols[...] + SC - from_columns(parts, 0, 2)
    reduce_columns(ktile, h, payload.at[0:16, :], kwide)


def step4_kernel(counts, idx, mine, other, plog_rows, ktile, tile, payload, tall, ktall):
    payload[...] = jnp.zeros(payload.shape, F32)
    h = plog_rows[...] + SC - fold_core(mine, other, 0, 2)
    reduce_rows(ktile, h, payload.at[0:8, :], ktall)
    live, h = fine_h(fold_core(mine, other, 16, 3), counts, idx, row_counts(counts, idx), 3)
    reduce_rows(tile, jnp.where(live, h, NEG), payload.at[8:20, :], tall)


def step5_kernel(counts, idx, p0, p1, p2, p3, plog_cols, members, tile, payload, coarse, tall, wide):
    z = idx[0]
    parts = (p0, p1, p2, p3)
    v = plog_cols[...] + SC - from_columns(parts, 0, 2)
    coarse[...] = v[0:1, :] * (1.0 / SC)
    to_rows(v, tall)
    ids = members[...].astype(jnp.int32)
    turn = lax.rem(z + Z - lax.shift_right_logical(ids, 11), Z)
    local = turn * (PROTO_BLOCK // Z) + jnp.bitwise_and(ids, PROTO_BLOCK // Z - 1)
    boost = []
    for k in range(X * 3):
        vals = tall[(k // 3) * PROTO_BLOCK:(k // 3 + 1) * PROTO_BLOCK, :]
        pick = iota((PROTO_BLOCK, 128), 0) == local[k:k + 1, :]
        boost.append(jnp.sum(jnp.where(pick, vals, 0.0), axis=0, keepdims=True))
    live, h = fine_h(from_columns(parts, 8, 3), counts, idx, col_counts(counts, idx), 3)
    h = jnp.where(live, h + jnp.concatenate(boost, axis=0), NEG)
    payload[...] = jnp.zeros(payload.shape, F32)
    reduce_columns(tile, h, payload, wide)


def step6_kernel(counts, idx, mine, other, tile, payload, out, tall):
    live, h = fine_h(fold_core(mine, other, 0, 3), counts, idx, row_counts(counts, idx), 3)
    out[...] = jnp.where(live, h, 0.0)[0:3, :] * (1.0 / SC)
    payload[...] = jnp.zeros(payload.shape, F32)
    reduce_rows(tile, jnp.where(live, h, NEG), payload, tall)


def last_kernel(counts, idx, p0, p1, p2, p3, out):
    parts = (p0, p1, p2, p3)
    live, h = fine_h(from_columns(parts, 0, 3), counts, idx, col_counts(counts, idx), 3)
    out[...] = jnp.where(live, h, 0.0)[0:3, :] * (1.0 / SC)


def hop(v, axis, k):
    n = {"x": X, "y": Y, "z": Z, "c": 2}[axis]
    return lax.ppermute(v, axis, [(i, (i + k) % n) for i in range(n)])


def spread_over(v, axis):
    return [v] + [hop(v, axis, k) for k in (1, 2, 3)]


def ring_start(v, axis):
    return hop(v, axis, 1), hop(v, axis, 3)


def ring_end(a, b, axis):
    half = a.shape[0] // 2
    return hop(a[:half], axis, 1), hop(b[half:], axis, 3)


def local(embeddings, members, counts):
    rows, d = embeddings.shape
    idx = jnp.stack([lax.axis_index(a) for a in ("z", "x", "y", "c")]).astype(jnp.int32)
    lanes = members.reshape(1, rows)
    lanes3 = members.reshape(rows // 128, 128)
    n_rows, n_cols = rows * Y * 2, rows * X
    k_rows, k_cols = PROTO_BLOCK * Y * 2, PROTO_BLOCK * X
    quarter = PROTO_BLOCK // Z

    xa, xb = ring_start(embeddings, "x")
    ya, yb = ring_start(embeddings, "y")
    so = hop(embeddings, "c", 1)
    own, far1, far2, far3 = call(
        pool_kernel,
        [sds((quarter, d + PAD))] + [sds((quarter, d + PAD), BF16)] * 3,
        [SMEM, SMEM, VMEM, VMEM],
        name="pool",
    )(counts, idx, embeddings, lanes)
    got = [hop(far1, "z", 1), hop(far2, "z", 2), hop(far3, "z", 3)]
    part = call(means_kernel, sds((quarter, d + PAD), BF16), [VMEM] * 4, name="means")(own, *got)
    means, plog = call(
        join_kernel, [sds((PROTO_BLOCK, d), BF16), sds((8, 128))], [SMEM] + [VMEM] * 4, name="join"
    )(counts, *spread_over(part, "z"))

    mxa, mxb = ring_start(means, "x")
    mya, myb = ring_start(means, "y")
    mso = hop(means, "c", 1)
    mxc, mxd = ring_end(mxa, mxb, "x")
    myc, myd = ring_end(mya, myb, "y")
    msa, msb, msc, msd = [hop(v, "c", 1) for v in (mya, myb, myc, myd)]

    xc, xd = ring_end(xa, xb, "x")
    yc, yd = ring_end(ya, yb, "y")
    sa, sb, sc, sd = [hop(v, "c", 1) for v in (ya, yb, yc, yd)]

    ktile, part = call(
        coarse_tile_kernel,
        [pltpu.VMEM((k_rows, k_cols), F32), sds((24, 128))],
        [ANY] * 14 + [VMEM],
        scratch=[
            pltpu.VMEM((k_rows, d), BF16),
            pltpu.VMEM((k_cols, d), BF16),
            pltpu.SemaphoreType.DMA((2 * Y,)),
            pltpu.SemaphoreType.DMA((X,)),
            pltpu.VMEM((8, k_cols), F32),
        ],
        name="coarse_tile",
        flops=2 * k_rows * k_cols * d,
    )(means, mxa, mxb, mxc, mxd, mya, myb, myc, myd, mso, msa, msb, msc, msd, plog)
    mine = call(
        lambda *r: fold_y_kernel({"lse": [(0, 2)], "plog": (16, 16)}, *r),
        sds((24, 128)),
        [VMEM] * 4,
        name="fold_y1",
    )(*spread_over(part, "y"))
    other = hop(mine, "c", 1)

    tile, upart = call(
        fine_tile_kernel,
        [pltpu.VMEM((n_rows, n_cols), F32), sds((n_cols // 128, 128))],
        [SMEM, SMEM] + [ANY] * 14,
        scratch=[
            pltpu.VMEM((n_rows, d), BF16),
            pltpu.VMEM((n_cols, d), BF16),
            pltpu.SemaphoreType.DMA((2 * Y,)),
            pltpu.SemaphoreType.DMA((X,)),
            pltpu.VMEM((n_rows, 128), F32),
            pltpu.VMEM((8, n_cols), F32),
        ],
        name="fine_tile",
        flops=2 * n_rows * n_cols * d,
    )(counts, idx, embeddings, xa, xb, xc, xd, ya, yb, yc, yd, so, sa, sb, sc, sd)

    tall = pltpu.VMEM((n_rows, 128), F32)
    wide = pltpu.VMEM((8, n_cols), F32)
    part, plog_rows = call(
        coarse2_kernel,
        [sds((32, 128)), sds((16, 128))],
        [VMEM] * 6,
        scratch=[pltpu.VMEM((k_rows, 128), F32)],
        name="coarse2",
    )(mine, other, upart, plog, lanes3, ktile)

    part, plog_cols, ids = call(
        step3_kernel,
        [sds((40, 128)), sds((8, 128)), sds((12, 128))],
        [SMEM, SMEM] + [VMEM] * 6,
        scratch=[wide, pltpu.VMEM((8, k_cols), F32)],
        name="step3",
    )(counts, idx, *spread_over(part, "x"), ktile, tile)
    mine = call(
        lambda *r: fold_y_kernel({"lse": [(0, 2), (16, 3)], "plog": None}, *r),
        sds((40, 128)),
        [VMEM] * 4,
        name="fold_y2",
    )(*spread_over(part, "y"))
    other = hop(mine, "c", 1)

    part = call(
        step4_kernel,
        sds((24, 128)),
        [SMEM, SMEM] + [VMEM] * 5,
        scratch=[tall, pltpu.VMEM((k_rows, 128), F32)],
        name="step4",
    )(counts, idx, mine, other, plog_rows, ktile, tile)

    part, coarse = call(
        step5_kernel,
        [sds((24, 128)), sds((1, 128))],
        [SMEM, SMEM] + [VMEM] * 7,
        scratch=[pltpu.VMEM((k_cols, 128), F32), wide],
        name="step5",
    )(counts, idx, *spread_over(part, "x"), plog_cols, ids, tile)
    mine = call(
        lambda *r: fold_y_kernel({"lse": [(0, 3)], "plog": None}, *r),
        sds((24, 128)),
        [VMEM] * 4,
        name="fold_y3",
    )(*spread_over(part, "y"))
    other = hop(mine, "c", 1)

    part, col = call(
        step6_kernel,
        [sds((16, 128)), sds((3, 128))],
        [SMEM, SMEM] + [VMEM] * 3,
        scratch=[tall],
        name="step6",
    )(counts, idx, mine, other, tile)
    row = call(last_kernel, sds((3, 128)), [SMEM, SMEM] + [VMEM] * 4, name="last")(
        counts, idx, *spread_over(part, "x")
    )
    return row.reshape(rows), col.reshape(rows), coarse[0, :quarter]


def solution(mesh):
    split = Mesh(mesh.devices.reshape(Z, X, Y, 2), ("z", "x", "y", "c"))
    every = P(("z", "x", "y", "c"))
    return jax.shard_map(
        local,
        mesh=split,
        in_specs=(P(("z", "x", "y", "c"), None), every, P()),
        out_specs=(every, every, every),
        check_vma=False,
    )
```

time: 547 us -> 202 us (0.37); the launches traced: 536 us -> 201 us
  blocking collectives: 308 us -> 0 us
  other arithmetic: 122 us -> 0.08 us
  Pallas kernels: 0 us -> 55.5 us
  starting transfers between devices: 0.12 us -> 54.8 us
  matrix products: 28 us -> 0 us
  local copies, waits for them, and re-layouts: 4.17 us -> 25.9 us
  between operations: 16.8 us -> 0.97 us
  waiting for transfers between devices: 57.6 us -> 64.1 us
    unnamed x5 -> x0, blocking collectives: 216 us -> none
    all_gather x4 -> x0, blocking collectives: 92 us -> none  [pull(): return lax.all_gather(h_loc, 'shard', axis=0, tiled=True)]
    ppermute x0 -> x53, waiting for transfers between devices: none -> 64.1 us  [hop(): return lax.ppermute(v, axis, [(i, (i + k) % n) for i in range(n)])]
    reduce_sum x12 -> x0, other arithmetic: 56.8 us -> none  [the longest x5 51.7 us: update_rows(): total = jnp.sum(jnp.exp(scores - top[:, None]), axis=1)]
    pallas_call x0 -> x14, Pallas kernels: none -> 55.5 us  [the longest x1 12.4 us: local(): call(fine_tile_kernel, [pltpu.VMEM((n_rows, n_cols), F32), sds((n_cols //...]
    ppermute x0 -> x53, starting transfers between devices: none -> 54.8 us  [hop(): return lax.ppermute(v, axis, [(i, (i + k) % n) for i in range(n)])]
    all_gather x2 -> x0, waiting for transfers between devices: 45.8 us -> none  [the longest x1 45.7 us: local(): piece = lax.all_gather(means, ('group', 'shard'), axis=0, tiled=True)]
    reduce_max x7 -> x0, other arithmetic: 35.4 us -> none  [the longest x4 34.5 us: update_rows(): top = jnp.max(scores, axis=1)]
  transfers between devices with their start and end apart: 3 -> 53, of which waited for: 2 -> 31; matrix products, arithmetic and copies ran while one was open for 8% -> 0% of each run, Pallas kernels for 0% -> 12%
where the time goes in v1:
time: 202 us; the launch traced here: 201 us
  waiting for transfers between devices  64.1 us (32%)
  Pallas kernels  55.5 us (27%)
  starting transfers between devices  54.8 us (27%)
  local copies, waits for them, and re-layouts  25.9 us (13%)
    ppermute x53, waiting for transfers between devices, hop(): return lax.ppermute(v, axis, [(i, (i + k) % n) for i in range(n)])  64.1 us
    ppermute x53, starting transfers between devices, hop(): return lax.ppermute(v, axis, [(i, (i + k) % n) for i in range(n)])  54.8 us
    unnamed x30, local copies, waits for them, and re-layouts  24.6 us
    pallas_call x1, Pallas kernels, local(): call(fine_tile_kernel, [pltpu.VMEM((n_rows, n_cols), F32), sds((n_cols //...  12.4 us
    pallas_call x1, Pallas kernels, local(): call(coarse_tile_kernel, [pltpu.VMEM((k_rows, k_cols), F32), sds((24, 128...  10.4 us
    pallas_call x1, Pallas kernels, local(): call(step4_kernel, sds((24, 128)), [SMEM, SMEM] + [VMEM] * 5, scratch=[ta...  8.33 us
    pallas_call x1, Pallas kernels, local(): call(step3_kernel, [sds((40, 128)), sds((8, 128)), sds((12, 128))], [SMEM...  6.76 us
    pallas_call x1, Pallas kernels, local(): call(step6_kernel, [sds((16, 128)), sds((3, 128))], [SMEM, SMEM] + [VMEM]...  6.36 us
  transfers between devices with their start and end apart: 53, of which 31 were waited for; matrix products, arithmetic and copies ran while one was open for 0% of the time, Pallas kernels for 12%

profile of v1, /device:TPU:0, one launch (start us, length us, event | category | flops | bytes accessed | tf_op | source)
XLA Modules:
  0.0 201.3 jit_solution(13587247622377931507)
XLA Ops:
  2.1 1.5 pool.1
  3.6 2.1 %collective-permute-start = (bf16[64,896]{1,0:T(8,128)(2,1)S(1)}, bf16[64,896]{1,0:T(8,128)(2,1)S(1)}, u32[]{:S(2)}, u32[]{:S(2)}) collective-permute-start(bf16[64,896]{1,0:T(8,128)(2,1)S(1)} %get-tuple-element.23), channel_id=1, source_target_pairs={{0,32},{32,64},{64,96},{96,0},{1,33},{33,65},{65,97},{97,1},{2,34}... | collective-permute-start | bytes 344072 | tf_op jit(solution)/shard_map/ppermute | solution.py:483
  5.7 3.6 %collective-permute-start.1 = (bf16[64,896]{1,0:T(8,128)(2,1)S(1)}, bf16[64,896]{1,0:T(8,128)(2,1)S(1)}, u32[]{:S(2)}, u32[]{:S(2)}) collective-permute-start(bf16[64,896]{1,0:T(8,128)(2,1)S(1)} %get-tuple-element.24), channel_id=1, source_target_pairs={{0,64},{32,96},{64,0},{96,32},{1,65},{33,97},{65,1},{97,33},{2,66}... | collective-permute-start | bytes 344072 | tf_op jit(solution)/shard_map/ppermute | solution.py:483
  10.2 3.0 %collective-permute-start.28 = (bf16[384,768]{1,0:T(8,128)(2,1)}, bf16[384,768]{1,0:T(8,128)(2,1)S(1)}, u32[]{:S(2)}, u32[]{:S(2)}) collective-permute-start(bf16[384,768]{1,0:T(8,128)(2,1)} %own.1), channel_id=1, source_target_pairs={{0,6},{2,0},{4,2},{6,4},{1,7},{3,1},{5,3},{7,5},{8,14},{10,8},{12,... | collective-permute-start | bytes 1769480 | tf_op jit(solution)/shard_map/ppermute | solution.py:483
  13.3 1.3 collective-permute-done.1.far2
  14.7 2.2 %collective-permute-start.5 = (bf16[64,896]{1,0:T(8,128)(2,1)S(1)}, bf16[64,896]{1,0:T(8,128)(2,1)S(1)}, u32[]{:S(2)}, u32[]{:S(2)}) collective-permute-start(bf16[64,896]{1,0:T(8,128)(2,1)S(1)} %means.1.own), channel_id=1, source_target_pairs={{0,96},{32,0},{64,32},{96,64},{1,97},{33,1},{65,33},{97,65},{2,98}... | collective-permute-start | bytes 344072 | tf_op jit(solution)/shard_map/ppermute | solution.py:483
  18.5 2.9 %collective-permute-done.5.far3 = bf16[64,896]{1,0:T(8,128)(2,1)S(1)} collective-permute-done((bf16[64,896]{1,0:T(8,128)(2,1)S(1)}, bf16[64,896]{1,0:T(8,128)(2,1)S(1)}, u32[]{:S(2)}, u32[]{:S(2)}) %collective-permute-start.5) | collective-permute-done | bytes 114720 | tf_op jit(solution)/shard_map/ppermute | solution.py:483
  21.3 2.5 %collective-permute-done.4.far2 = bf16[64,896]{1,0:T(8,128)(2,1)S(1)} collective-permute-done((bf16[64,896]{1,0:T(8,128)(2,1)S(1)}, bf16[64,896]{1,0:T(8,128)(2,1)S(1)}, u32[]{:S(2)}, u32[]{:S(2)}) %collective-permute-start.4) | collective-permute-done | bytes 114720 | tf_op jit(solution)/shard_map/ppermute | solution.py:483
  26.4 3.1 %collective-permute-start.11 = (bf16[256,768]{1,0:T(8,128)(2,1)S(1)}, bf16[256,768]{1,0:T(8,128)(2,1)S(1)}, u32[]{:S(2)}, u32[]{:S(2)}) collective-permute-start(bf16[256,768]{1,0:T(8,128)(2,1)S(1)} %get-tuple-element.26.own), channel_id=1, source_target_pairs={{0,6},{2,0},{4,2},{6,4},{1,7},{3,1},{5,3},{7,5},{8,14},{10,8},{12,... | collective-permute-start | bytes 1179656 | tf_op jit(solution)/shard_map/ppermute | solution.py:483
  29.5 2.8 %collective-permute-start.7 = (bf16[256,768]{1,0:T(8,128)(2,1)S(1)}, bf16[256,768]{1,0:T(8,128)(2,1)S(1)}, u32[]{:S(2)}, u32[]{:S(2)}) collective-permute-start(bf16[256,768]{1,0:T(8,128)(2,1)S(1)} %get-tuple-element.26.own), channel_id=1, source_target_pairs={{0,24},{8,0},{16,8},{24,16},{1,25},{9,1},{17,9},{25,17},{2,26},{10... | collective-permute-start | bytes 1179656 | tf_op jit(solution)/shard_map/ppermute | solution.py:483
  34.3 1.8 collective-permute-done.11.refs_5_
  36.1 3.4 %collective-permute-done.10.refs_4_ = bf16[256,768]{1,0:T(8,128)(2,1)S(1)} collective-permute-done((bf16[256,768]{1,0:T(8,128)(2,1)S(1)}, bf16[256,768]{1,0:T(8,128)(2,1)S(1)}, u32[]{:S(2)}, u32[]{:S(2)}) %collective-permute-start.10) | collective-permute-done | bytes 393248 | tf_op jit(solution)/shard_map/ppermute | solution.py:483
  39.5 2.3 %collective-permute-done.7.refs_1_ = bf16[256,768]{1,0:T(8,128)(2,1)S(1)} collective-permute-done((bf16[256,768]{1,0:T(8,128)(2,1)S(1)}, bf16[256,768]{1,0:T(8,128)(2,1)S(1)}, u32[]{:S(2)}, u32[]{:S(2)}) %collective-permute-start.7) | collective-permute-done | bytes 393248 | tf_op jit(solution)/shard_map/ppermute | solution.py:483
  43.1 8.2 %collective-permute-done.24.refs_1_ = bf16[384,768]{1,0:T(8,128)(2,1)S(1)} collective-permute-done((bf16[384,768]{1,0:T(8,128)(2,1)}, bf16[384,768]{1,0:T(8,128)(2,1)S(1)}, u32[]{:S(2)}, u32[]{:S(2)}) %collective-permute-start.24) | collective-permute-done | bytes 589856 | tf_op jit(solution)/shard_map/ppermute | solution.py:483
  51.4 3.0 %collective-permute-start.13 = (bf16[128,768]{1,0:T(8,128)(2,1)S(1)}, bf16[128,768]{1,0:T(8,128)(2,1)S(1)}, u32[]{:S(2)}, u32[]{:S(2)}) collective-permute-start(bf16[128,768]{1,0:T(8,128)(2,1)S(1)} %slice.39), channel_id=1, source_target_pairs={{0,6},{2,0},{4,2},{6,4},{1,7},{3,1},{5,3},{7,5},{8,14},{10,8},{12,... | collective-permute-start | bytes 589832 | tf_op jit(solution)/shard_map/ppermute | solution.py:483
  54.4 3.7 %collective-permute-start.9 = (bf16[128,768]{1,0:T(8,128)(2,1)S(1)}, bf16[128,768]{1,0:T(8,128)(2,1)S(1)}, u32[]{:S(2)}, u32[]{:S(2)}) collective-permute-start(bf16[128,768]{1,0:T(8,128)(2,1)S(1)} %slice.37), channel_id=1, source_target_pairs={{0,24},{8,0},{16,8},{24,16},{1,25},{9,1},{17,9},{25,17},{2,26},{10... | collective-permute-start | bytes 589832 | tf_op jit(solution)/shard_map/ppermute | solution.py:483
  58.6 2.6 %collective-permute-done.12.refs_6_ = bf16[128,768]{1,0:T(8,128)(2,1)S(1)} collective-permute-done((bf16[128,768]{1,0:T(8,128)(2,1)S(1)}, bf16[128,768]{1,0:T(8,128)(2,1)S(1)}, u32[]{:S(2)}, u32[]{:S(2)}) %collective-permute-start.12) | collective-permute-done | bytes 196640 | tf_op jit(solution)/shard_map/ppermute | solution.py:483
  61.2 1.6 collective-permute-done.9.refs_3_
  62.9 3.8 %collective-permute-done.8.refs_2_ = bf16[128,768]{1,0:T(8,128)(2,1)S(1)} collective-permute-done((bf16[128,768]{1,0:T(8,128)(2,1)S(1)}, bf16[128,768]{1,0:T(8,128)(2,1)S(1)}, u32[]{:S(2)}, u32[]{:S(2)}) %collective-permute-start.8) | collective-permute-done | bytes 196640 | tf_op jit(solution)/shard_map/ppermute | solution.py:483
  66.7 3.1 %collective-permute-start.30 = (bf16[192,768]{1,0:T(8,128)(2,1)S(1)}, bf16[192,768]{1,0:T(8,128)(2,1)S(1)}, u32[]{:S(2)}, u32[]{:S(2)}) collective-permute-start(bf16[192,768]{1,0:T(8,128)(2,1)S(1)} %slice.43), channel_id=1, source_target_pairs={{0,6},{2,0},{4,2},{6,4},{1,7},{3,1},{5,3},{7,5},{8,14},{10,8},{12,... | collective-permute-start | bytes 884744 | tf_op jit(solution)/shard_map/ppermute | solution.py:483
  71.0 10.4 %coarse_tile.1 = (f32[2048,1024]{1,0:T(8,128)S(1)}, f32[24,128]{1,0:T(8,128)S(1)}) custom-call(bf16[256,768]{1,0:T(8,128)(2,1)S(1)} %get-tuple-element.26.own, bf16[256,768]{1,0:T(8,128)(2,1)S(1)} %collective-permute-done.6.refs_0_, bf16[256,768]{1,0:T(8,128)(2,1)S(1)} %collective-permute-done.7.refs_1_, ...), custom_call_target="tpu_custom_call" | custom-call | flops 3221225472 | tf_op jit(solution)/shard_map/coarse_tile/pallas_call | solution.py:534
  81.5 3.2 %collective-permute-start.21 = (f32[24,128]{1,0:T(8,128)S(1)}, f32[24,128]{1,0:T(8,128)S(1)}, u32[]{:S(2)}, u32[]{:S(2)}) collective-permute-start(f32[24,128]{1,0:T(8,128)S(1)} %get-tuple-element.28.r_0_), channel_id=1, source_target_pairs={{0,6},{2,0},{4,2},{6,4},{1,7},{3,1},{5,3},{7,5},{8,14},{10,8},{12,... | collective-permute-start | bytes 36872 | tf_op jit(solution)/shard_map/ppermute | solution.py:483
  86.1 1.4 collective-permute-start.25
  87.6 2.4 %collective-permute-done.20.r_2_ = f32[24,128]{1,0:T(8,128)S(1)} collective-permute-done((f32[24,128]{1,0:T(8,128)S(1)}, f32[24,128]{1,0:T(8,128)S(1)}, u32[]{:S(2)}, u32[]{:S(2)}) %collective-permute-start.20) | collective-permute-done | bytes 12320 | tf_op jit(solution)/shard_map/ppermute | solution.py:483
  90.5 5.0 %collective-permute-done.25.refs_2_ = bf16[192,768]{1,0:T(8,128)(2,1)S(1)} collective-permute-done((bf16[192,768]{1,0:T(8,128)(2,1)S(1)}, bf16[192,768]{1,0:T(8,128)(2,1)S(1)}, u32[]{:S(2)}, u32[]{:S(2)}) %collective-permute-start.25) | collective-permute-done | bytes 294944 | tf_op jit(solution)/shard_map/ppermute | solution.py:483
  96.2 12.4 %fine_tile.1 = (f32[3072,1536]{1,0:T(8,128)S(1)}, f32[12,128]{1,0:T(8,128)S(1)}) custom-call(s32[4,32]{1,0:T(4,128)S(1)} %copy-done.7, s32[4]{0:T(128)S(1)} %pad_add_fusion.idx, bf16[384,768]{1,0:T(8,128)(2,1)} %own.1, bf16[384,768]{1,0:T(8,128)(2,1)S(1)} %collective-permute-done.23.refs_0_, bf16[384,768]{1,0:T(8,128)(2,1)S(1)} %collective-permute-done.24.refs_1_, ...), custom_call_target="tpu_custom_call" | custom-call | flops 7247757312 | tf_op jit(solution)/shard_map/fine_tile/pallas_call | solution.py:556
  108.7 6.4 %copy-done = f32[3072,1536]{1,0:T(8,128)} copy-done((f32[3072,1536]{1,0:T(8,128)}, f32[3072,1536]{1,0:T(8,128)S(1)}, u32[]{:S(2)}) %copy-start) | copy-done | bytes 18874392
  115.1 2.5 %coarse2.1 = (f32[32,128]{1,0:T(8,128)S(1)}, f32[16,128]{1,0:T(8,128)S(1)}) custom-call(f32[24,128]{1,0:T(8,128)S(1)} %fold_y1.1.mine, f32[24,128]{1,0:T(8,128)S(1)} %collective-permute-done.22.other, f32[12,128]{1,0:T(8,128)S(1)} %get-tuple-element.29.part, f32[8,128]{1,0:T(8,128)S(1)} %get-tuple-element.27.refs_13_.plog, s32[3,128]{1,0:T(4,128)S(1)} %bitcast.11, ...), custom_call_target="tpu_custom_call" | custom-call | tf_op jit(solution)/shard_map/coarse2/pallas_call | solution.py:574
  117.7 2.3 %collective-permute-start.37 = (f32[32,128]{1,0:T(8,128)S(1)}, f32[32,128]{1,0:T(8,128)S(1)}, u32[]{:S(2)}, u32[]{:S(2)}) collective-permute-start(f32[32,128]{1,0:T(8,128)S(1)} %get-tuple-element.31.p0), channel_id=1, source_target_pairs={{0,16},{8,24},{16,0},{24,8},{1,17},{9,25},{17,1},{25,9},{2,18},{10... | collective-permute-start | bytes 49160 | tf_op jit(solution)/shard_map/ppermute | solution.py:483
  120.0 1.4 collective-permute-done.38.p3
  121.4 1.6 collective-permute-done.37.p2
  123.0 1.9 collective-permute-done.36.p1
  124.9 6.4 %copy-done.1 = f32[3072,1536]{1,0:T(8,128)S(1)} copy-done((f32[3072,1536]{1,0:T(8,128)S(1)}, f32[3072,1536]{1,0:T(8,128)}, u32[]{:S(2)}) %copy-start.1) | copy-done | bytes 18874392
  131.3 6.8 %step3.1 = (f32[40,128]{1,0:T(8,128)S(1)}, f32[8,128]{1,0:T(8,128)S(1)}, f32[12,128]{1,0:T(8,128)S(1)}) custom-call(s32[4,32]{1,0:T(4,128)S(1)} %copy-done.8, s32[4]{0:T(128)S(1)} %pad_add_fusion.idx, f32[32,128]{1,0:T(8,128)S(1)} %get-tuple-element.31.p0, f32[32,128]{1,0:T(8,128)S(1)} %collective-permute-done.36.p1, ...), custom_call_target="tpu_custom_call" | custom-call | tf_op jit(solution)/shard_map/step3/pallas_call | solution.py:582
  138.1 3.3 %collective-permute-start.41 = (f32[40,128]{1,0:T(8,128)S(1)}, f32[40,128]{1,0:T(8,128)S(1)}, u32[]{:S(2)}, u32[]{:S(2)}) collective-permute-start(f32[40,128]{1,0:T(8,128)S(1)} %get-tuple-element.33.r_0_), channel_id=1, source_target_pairs={{0,6},{2,0},{4,2},{6,4},{1,7},{3,1},{5,3},{7,5},{8,14},{10,8},{12,... | collective-permute-start | bytes 61448 | tf_op jit(solution)/shard_map/ppermute | solution.py:483
  142.8 3.8 %collective-permute-done.40.r_2_ = f32[40,128]{1,0:T(8,128)S(1)} collective-permute-done((f32[40,128]{1,0:T(8,128)S(1)}, f32[40,128]{1,0:T(8,128)S(1)}, u32[]{:S(2)}, u32[]{:S(2)}) %collective-permute-start.40) | collective-permute-done | bytes 20512 | tf_op jit(solution)/shard_map/ppermute | solution.py:483
  148.8 3.4 %copy-done.4 = f32[2048,1024]{1,0:T(8,128)S(1)} copy-done((f32[2048,1024]{1,0:T(8,128)S(1)}, f32[2048,1024]{1,0:T(8,128)}, u32[]{:S(2)}) %copy-start.4) | copy-done | bytes 8388632
  152.1 8.3 %step4.1.p0 = f32[24,128]{1,0:T(8,128)S(1)} custom-call(s32[4,32]{1,0:T(4,128)S(1)} %copy-done.8, s32[4]{0:T(128)S(1)} %pad_add_fusion.idx, f32[40,128]{1,0:T(8,128)S(1)} %fold_y2.1.mine, f32[40,128]{1,0:T(8,128)S(1)} %collective-permute-done.42.other, f32[16,128]{1,0:T(8,128)S(1)} %get-tuple-element.34.plog_rows, f32[2048,1024]{1,0:T(8,128)S(1)} %copy-done.4, ...), custom_call_target="tpu_custom_call" | custom-call | tf_op jit(solution)/shard_map/step4/pallas_call | solution.py:597
  162.7 1.5 collective-permute-done.45.p3
  164.2 2.8 %collective-permute-done.44.p2 = f32[24,128]{1,0:T(8,128)S(1)} collective-permute-done((f32[24,128]{1,0:T(8,128)S(1)}, f32[24,128]{1,0:T(8,128)S(1)}, u32[]{:S(2)}, u32[]{:S(2)}) %collective-permute-start.44) | collective-permute-done | bytes 12320 | tf_op jit(solution)/shard_map/ppermute | solution.py:483
  167.6 6.4 %copy-done.2 = f32[3072,1536]{1,0:T(8,128)S(1)} copy-done((f32[3072,1536]{1,0:T(8,128)S(1)}, f32[3072,1536]{1,0:T(8,128)}, u32[]{:S(2)}) %copy-start.2) | copy-done | bytes 18874392
  173.9 4.9 %step5.1 = (f32[24,128]{1,0:T(8,128)S(1)}, f32[1,128]{1,0:T(1,128)S(1)}) custom-call(s32[4,32]{1,0:T(4,128)S(1)} %copy-done.8, s32[4]{0:T(128)S(1)} %pad_add_fusion.idx, f32[24,128]{1,0:T(8,128)S(1)} %step4.1.p0, f32[24,128]{1,0:T(8,128)S(1)} %collective-permute-done.43.p1, f32[24,128]{1,0:T(8,128)S(1)} %collective-permute-done.44.p2, ...), custom_call_target="tpu_custom_call" | custom-call | tf_op jit(solution)/shard_map/step5/pallas_call | solution.py:605
  178.9 1.3 collective-permute-start.47
  180.2 1.3 collective-permute-start.46
  182.6 1.6 collective-permute-done.47.r_2_
  186.6 6.4 %step6.1 = (f32[16,128]{1,0:T(8,128)S(1)}, f32[3,128]{1,0:T(4,128)}) custom-call(s32[4,32]{1,0:T(4,128)S(1)} %copy-done.8, s32[4]{0:T(128)S(1)} %pad_add_fusion.idx, f32[24,128]{1,0:T(8,128)S(1)} %fold_y3.1.mine, f32[24,128]{1,0:T(8,128)S(1)} %collective-permute-done.49.other, f32[3072,1536]{1,0:T(8,128)S(1)} %bitcast.10), custom_call_target="tpu_custom_call" | custom-call | tf_op jit(solution)/shard_map/step6/pallas_call | solution.py:620
  193.0 1.4 collective-permute-start.52
  196.6 2.9 %collective-permute-done.51.p2 = f32[16,128]{1,0:T(8,128)S(1)} collective-permute-done((f32[16,128]{1,0:T(8,128)S(1)}, f32[16,128]{1,0:T(8,128)S(1)}, u32[]{:S(2)}, u32[]{:S(2)}) %collective-permute-start.51) | collective-permute-done | bytes 8224 | tf_op jit(solution)/shard_map/ppermute | solution.py:483
  (114 shorter events, 28.6 us)
Async XLA Ops:
  3.6 9.7 %collective-permute-start = (bf16[64,896]{1,0:T(8,128)(2,1)S(1)}, bf16[64,896]{1,0:T(8,128)(2,1)S(1)}, u32[]{:S(2)}, u32[]{:S(2)}) collective-permute-start(bf16[64,896]{1,0:T(8,128)(2,1)S(1)} %get-tuple-element.23), channel_id=1, source_target_pairs={{0,32},{32,64},{64,96},{96,0},{1,33},{33,65},{65,97},{97,1},{2,34}... | collective-permute-start | bytes 344072 | tf_op jit(solution)/shard_map/ppermute | solution.py:483
  5.7 8.9 %collective-permute-start.1 = (bf16[64,896]{1,0:T(8,128)(2,1)S(1)}, bf16[64,896]{1,0:T(8,128)(2,1)S(1)}, u32[]{:S(2)}, u32[]{:S(2)}) collective-permute-start(bf16[64,896]{1,0:T(8,128)(2,1)S(1)} %get-tuple-element.24), channel_id=1, source_target_pairs={{0,64},{32,96},{64,0},{96,32},{1,65},{33,97},{65,1},{97,33},{2,66}... | collective-permute-start | bytes 344072 | tf_op jit(solution)/shard_map/ppermute | solution.py:483
  9.2 5.3 %collective-permute-start.2 = (bf16[64,896]{1,0:T(8,128)(2,1)S(1)}, bf16[64,896]{1,0:T(8,128)(2,1)S(1)}, u32[]{:S(2)}, u32[]{:S(2)}) collective-permute-start(bf16[64,896]{1,0:T(8,128)(2,1)S(1)} %get-tuple-element.25), channel_id=1, source_target_pairs={{0,96},{32,0},{64,32},{96,64},{1,97},{33,1},{65,33},{97,65},{2,98}... | collective-permute-start | bytes 344072 | tf_op jit(solution)/shard_map/ppermute | solution.py:483
  10.2 22.0 %collective-permute-start.28 = (bf16[384,768]{1,0:T(8,128)(2,1)}, bf16[384,768]{1,0:T(8,128)(2,1)S(1)}, u32[]{:S(2)}, u32[]{:S(2)}) collective-permute-start(bf16[384,768]{1,0:T(8,128)(2,1)} %own.1), channel_id=1, source_target_pairs={{0,6},{2,0},{4,2},{6,4},{1,7},{3,1},{5,3},{7,5},{8,14},{10,8},{12,... | collective-permute-start | bytes 1769480 | tf_op jit(solution)/shard_map/ppermute | solution.py:483
  13.3 19.8 %collective-permute-start.27 = (bf16[384,768]{1,0:T(8,128)(2,1)}, bf16[384,768]{1,0:T(8,128)(2,1)S(1)}, u32[]{:S(2)}, u32[]{:S(2)}) collective-permute-start(bf16[384,768]{1,0:T(8,128)(2,1)} %own.1), channel_id=1, source_target_pairs={{0,2},{2,4},{4,6},{6,0},{1,3},{3,5},{5,7},{7,1},{8,10},{10,12},{12... | collective-permute-start | bytes 1769480 | tf_op jit(solution)/shard_map/ppermute | solution.py:483
  14.7 6.6 %collective-permute-start.5 = (bf16[64,896]{1,0:T(8,128)(2,1)S(1)}, bf16[64,896]{1,0:T(8,128)(2,1)S(1)}, u32[]{:S(2)}, u32[]{:S(2)}) collective-permute-start(bf16[64,896]{1,0:T(8,128)(2,1)S(1)} %means.1.own), channel_id=1, source_target_pairs={{0,96},{32,0},{64,32},{96,64},{1,97},{33,1},{65,33},{97,65},{2,98}... | collective-permute-start | bytes 344072 | tf_op jit(solution)/shard_map/ppermute | solution.py:483
  17.0 6.9 %collective-permute-start.4 = (bf16[64,896]{1,0:T(8,128)(2,1)S(1)}, bf16[64,896]{1,0:T(8,128)(2,1)S(1)}, u32[]{:S(2)}, u32[]{:S(2)}) collective-permute-start(bf16[64,896]{1,0:T(8,128)(2,1)S(1)} %means.1.own), channel_id=1, source_target_pairs={{0,64},{32,96},{64,0},{96,32},{1,65},{33,97},{65,1},{97,33},{2,66}... | collective-permute-start | bytes 344072 | tf_op jit(solution)/shard_map/ppermute | solution.py:483
  18.1 6.9 %collective-permute-start.3 = (bf16[64,896]{1,0:T(8,128)(2,1)S(1)}, bf16[64,896]{1,0:T(8,128)(2,1)S(1)}, u32[]{:S(2)}, u32[]{:S(2)}) collective-permute-start(bf16[64,896]{1,0:T(8,128)(2,1)S(1)} %means.1.own), channel_id=1, source_target_pairs={{0,32},{32,64},{64,96},{96,0},{1,33},{33,65},{65,97},{97,1},{2,34}... | collective-permute-start | bytes 344072 | tf_op jit(solution)/shard_map/ppermute | solution.py:483
  26.4 9.7 %collective-permute-start.11 = (bf16[256,768]{1,0:T(8,128)(2,1)S(1)}, bf16[256,768]{1,0:T(8,128)(2,1)S(1)}, u32[]{:S(2)}, u32[]{:S(2)}) collective-permute-start(bf16[256,768]{1,0:T(8,128)(2,1)S(1)} %get-tuple-element.26.own), channel_id=1, source_target_pairs={{0,6},{2,0},{4,2},{6,4},{1,7},{3,1},{5,3},{7,5},{8,14},{10,8},{12,... | collective-permute-start | bytes 1179656 | tf_op jit(solution)/shard_map/ppermute | solution.py:483
  29.5 10.0 %collective-permute-start.10 = (bf16[256,768]{1,0:T(8,128)(2,1)S(1)}, bf16[256,768]{1,0:T(8,128)(2,1)S(1)}, u32[]{:S(2)}, u32[]{:S(2)}) collective-permute-start(bf16[256,768]{1,0:T(8,128)(2,1)S(1)} %get-tuple-element.26.own), channel_id=1, source_target_pairs={{0,2},{2,4},{4,6},{6,0},{1,3},{3,5},{5,7},{7,1},{8,10},{10,12},{12... | collective-permute-start | bytes 1179656 | tf_op jit(solution)/shard_map/ppermute | solution.py:483
  29.5 12.3 %collective-permute-start.7 = (bf16[256,768]{1,0:T(8,128)(2,1)S(1)}, bf16[256,768]{1,0:T(8,128)(2,1)S(1)}, u32[]{:S(2)}, u32[]{:S(2)}) collective-permute-start(bf16[256,768]{1,0:T(8,128)(2,1)S(1)} %get-tuple-element.26.own), channel_id=1, source_target_pairs={{0,24},{8,0},{16,8},{24,16},{1,25},{9,1},{17,9},{25,17},{2,26},{10... | collective-permute-start | bytes 1179656 | tf_op jit(solution)/shard_map/ppermute | solution.py:483
  32.3 19.1 %collective-permute-start.24 = (bf16[384,768]{1,0:T(8,128)(2,1)}, bf16[384,768]{1,0:T(8,128)(2,1)S(1)}, u32[]{:S(2)}, u32[]{:S(2)}) collective-permute-start(bf16[384,768]{1,0:T(8,128)(2,1)} %own.1), channel_id=1, source_target_pairs={{0,24},{8,0},{16,8},{24,16},{1,25},{9,1},{17,9},{25,17},{2,26},{10... | collective-permute-start | bytes 1769480 | tf_op jit(solution)/shard_map/ppermute | solution.py:483
  33.1 21.2 %collective-permute-start.23 = (bf16[384,768]{1,0:T(8,128)(2,1)}, bf16[384,768]{1,0:T(8,128)(2,1)S(1)}, u32[]{:S(2)}, u32[]{:S(2)}) collective-permute-start(bf16[384,768]{1,0:T(8,128)(2,1)} %own.1), channel_id=1, source_target_pairs={{0,8},{8,16},{16,24},{24,0},{1,9},{9,17},{17,25},{25,1},{2,10},{10... | collective-permute-start | bytes 1769480 | tf_op jit(solution)/shard_map/ppermute | solution.py:483
  36.1 18.2 %collective-permute-start.31 = (bf16[384,768]{1,0:T(8,128)(2,1)}, bf16[384,768]{1,0:T(8,128)(2,1)S(1)}, u32[]{:S(2)}, u32[]{:S(2)}) collective-permute-start(bf16[384,768]{1,0:T(8,128)(2,1)} %own.1), channel_id=1, source_target_pairs={{0,1},{1,0},{2,3},{3,2},{4,5},{5,4},{6,7},{7,6},{8,9},{9,8},{10,11... | collective-permute-start | bytes 1769480 | tf_op jit(solution)/shard_map/ppermute | solution.py:483
  39.5 14.9 %collective-permute-start.14 = (bf16[256,768]{1,0:T(8,128)(2,1)S(1)}, bf16[256,768]{1,0:T(8,128)(2,1)S(1)}, u32[]{:S(2)}, u32[]{:S(2)}) collective-permute-start(bf16[256,768]{1,0:T(8,128)(2,1)S(1)} %get-tuple-element.26.own), channel_id=1, source_target_pairs={{0,1},{1,0},{2,3},{3,2},{4,5},{5,4},{6,7},{7,6},{8,9},{9,8},{10,11... | collective-permute-start | bytes 1179656 | tf_op jit(solution)/shard_map/ppermute | solution.py:483
  41.8 16.2 %collective-permute-start.6 = (bf16[256,768]{1,0:T(8,128)(2,1)S(1)}, bf16[256,768]{1,0:T(8,128)(2,1)S(1)}, u32[]{:S(2)}, u32[]{:S(2)}) collective-permute-start(bf16[256,768]{1,0:T(8,128)(2,1)S(1)} %get-tuple-element.26.own), channel_id=1, source_target_pairs={{0,8},{8,16},{16,24},{24,0},{1,9},{9,17},{17,25},{25,1},{2,10},{10... | collective-permute-start | bytes 1179656 | tf_op jit(solution)/shard_map/ppermute | solution.py:483
  51.4 6.9 %collective-permute-start.13 = (bf16[128,768]{1,0:T(8,128)(2,1)S(1)}, bf16[128,768]{1,0:T(8,128)(2,1)S(1)}, u32[]{:S(2)}, u32[]{:S(2)}) collective-permute-start(bf16[128,768]{1,0:T(8,128)(2,1)S(1)} %slice.39), channel_id=1, source_target_pairs={{0,6},{2,0},{4,2},{6,4},{1,7},{3,1},{5,3},{7,5},{8,14},{10,8},{12,... | collective-permute-start | bytes 589832 | tf_op jit(solution)/shard_map/ppermute | solution.py:483
  54.3 6.9 %collective-permute-start.12 = (bf16[128,768]{1,0:T(8,128)(2,1)S(1)}, bf16[128,768]{1,0:T(8,128)(2,1)S(1)}, u32[]{:S(2)}, u32[]{:S(2)}) collective-permute-start(bf16[128,768]{1,0:T(8,128)(2,1)S(1)} %slice.38), channel_id=1, source_target_pairs={{0,2},{2,4},{4,6},{6,0},{1,3},{3,5},{5,7},{7,1},{8,10},{10,12},{12... | collective-permute-start | bytes 589832 | tf_op jit(solution)/shard_map/ppermute | solution.py:483
  54.3 15.5 %collective-permute-start.16 = (bf16[256,768]{1,0:T(8,128)(2,1)S(1)}, bf16[256,768]{1,0:T(8,128)(2,1)S(1)}, u32[]{:S(2)}, u32[]{:S(2)}) collective-permute-start(bf16[256,768]{1,0:T(8,128)(2,1)S(1)} %collective-permute-done.11.refs_5_), channel_id=1, source_target_pairs={{0,1},{1,0},{2,3},{3,2},{4,5},{5,4},{6,7},{7,6},{8,9},{9,8},{10,11... | collective-permute-start | bytes 1179656 | tf_op jit(solution)/shard_map/ppermute | solution.py:483
  54.4 8.4 %collective-permute-start.9 = (bf16[128,768]{1,0:T(8,128)(2,1)S(1)}, bf16[128,768]{1,0:T(8,128)(2,1)S(1)}, u32[]{:S(2)}, u32[]{:S(2)}) collective-permute-start(bf16[128,768]{1,0:T(8,128)(2,1)S(1)} %slice.37), channel_id=1, source_target_pairs={{0,24},{8,0},{16,8},{24,16},{1,25},{9,1},{17,9},{25,17},{2,26},{10... | collective-permute-start | bytes 589832 | tf_op jit(solution)/shard_map/ppermute | solution.py:483
  58.1 12.5 %collective-permute-start.15 = (bf16[256,768]{1,0:T(8,128)(2,1)S(1)}, bf16[256,768]{1,0:T(8,128)(2,1)S(1)}, u32[]{:S(2)}, u32[]{:S(2)}) collective-permute-start(bf16[256,768]{1,0:T(8,128)(2,1)S(1)} %collective-permute-done.10.refs_4_), channel_id=1, source_target_pairs={{0,1},{1,0},{2,3},{3,2},{4,5},{5,4},{6,7},{7,6},{8,9},{9,8},{10,11... | collective-permute-start | bytes 1179656 | tf_op jit(solution)/shard_map/ppermute | solution.py:483
  58.3 8.4 %collective-permute-start.8 = (bf16[128,768]{1,0:T(8,128)(2,1)S(1)}, bf16[128,768]{1,0:T(8,128)(2,1)S(1)}, u32[]{:S(2)}, u32[]{:S(2)}) collective-permute-start(bf16[128,768]{1,0:T(8,128)(2,1)S(1)} %slice.36), channel_id=1, source_target_pairs={{0,8},{8,16},{16,24},{24,0},{1,9},{9,17},{17,25},{25,1},{2,10},{10... | collective-permute-start | bytes 589832 | tf_op jit(solution)/shard_map/ppermute | solution.py:483
  61.2 8.7 %collective-permute-start.18 = (bf16[128,768]{1,0:T(8,128)(2,1)S(1)}, bf16[128,768]{1,0:T(8,128)(2,1)S(1)}, u32[]{:S(2)}, u32[]{:S(2)}) collective-permute-start(bf16[128,768]{1,0:T(8,128)(2,1)S(1)} %collective-permute-done.13.refs_7_), channel_id=1, source_target_pairs={{0,1},{1,0},{2,3},{3,2},{4,5},{5,4},{6,7},{7,6},{8,9},{9,8},{10,11... | collective-permute-start | bytes 589832 | tf_op jit(solution)/shard_map/ppermute | solution.py:483
  62.8 7.7 %collective-permute-start.17 = (bf16[128,768]{1,0:T(8,128)(2,1)S(1)}, bf16[128,768]{1,0:T(8,128)(2,1)S(1)}, u32[]{:S(2)}, u32[]{:S(2)}) collective-permute-start(bf16[128,768]{1,0:T(8,128)(2,1)S(1)} %collective-permute-done.12.refs_6_), channel_id=1, source_target_pairs={{0,1},{1,0},{2,3},{3,2},{4,5},{5,4},{6,7},{7,6},{8,9},{9,8},{10,11... | collective-permute-start | bytes 589832 | tf_op jit(solution)/shard_map/ppermute | solution.py:483
  66.7 14.8 %collective-permute-start.30 = (bf16[192,768]{1,0:T(8,128)(2,1)S(1)}, bf16[192,768]{1,0:T(8,128)(2,1)S(1)}, u32[]{:S(2)}, u32[]{:S(2)}) collective-permute-start(bf16[192,768]{1,0:T(8,128)(2,1)S(1)} %slice.43), channel_id=1, source_target_pairs={{0,6},{2,0},{4,2},{6,4},{1,7},{3,1},{5,3},{7,5},{8,14},{10,8},{12,... | collective-permute-start | bytes 884744 | tf_op jit(solution)/shard_map/ppermute | solution.py:483
  69.8 14.9 %collective-permute-start.29 = (bf16[192,768]{1,0:T(8,128)(2,1)S(1)}, bf16[192,768]{1,0:T(8,128)(2,1)S(1)}, u32[]{:S(2)}, u32[]{:S(2)}) collective-permute-start(bf16[192,768]{1,0:T(8,128)(2,1)S(1)} %slice.42), channel_id=1, source_target_pairs={{0,2},{2,4},{4,6},{6,0},{1,3},{3,5},{5,7},{7,1},{8,10},{10,12},{12... | collective-permute-start | bytes 884744 | tf_op jit(solution)/shard_map/ppermute | solution.py:483
  69.9 14.9 %collective-permute-start.26 = (bf16[192,768]{1,0:T(8,128)(2,1)S(1)}, bf16[192,768]{1,0:T(8,128)(2,1)S(1)}, u32[]{:S(2)}, u32[]{:S(2)}) collective-permute-start(bf16[192,768]{1,0:T(8,128)(2,1)S(1)} %slice.41), channel_id=1, source_target_pairs={{0,24},{8,0},{16,8},{24,16},{1,25},{9,1},{17,9},{25,17},{2,26},{10... | collective-permute-start | bytes 884744 | tf_op jit(solution)/shard_map/ppermute | solution.py:483
  70.5 25.0 %collective-permute-start.33 = (bf16[384,768]{1,0:T(8,128)(2,1)S(1)}, bf16[384,768]{1,0:T(8,128)(2,1)S(1)}, u32[]{:S(2)}, u32[]{:S(2)}) collective-permute-start(bf16[384,768]{1,0:T(8,128)(2,1)S(1)} %collective-permute-done.28.refs_5_), channel_id=1, source_target_pairs={{0,1},{1,0},{2,3},{3,2},{4,5},{5,4},{6,7},{7,6},{8,9},{9,8},{10,11... | collective-permute-start | bytes 1769480 | tf_op jit(solution)/shard_map/ppermute | solution.py:483
  70.5 25.0 %collective-permute-start.32 = (bf16[384,768]{1,0:T(8,128)(2,1)S(1)}, bf16[384,768]{1,0:T(8,128)(2,1)S(1)}, u32[]{:S(2)}, u32[]{:S(2)}) collective-permute-start(bf16[384,768]{1,0:T(8,128)(2,1)S(1)} %collective-permute-done.27.refs_4_), channel_id=1, source_target_pairs={{0,1},{1,0},{2,3},{3,2},{4,5},{5,4},{6,7},{7,6},{8,9},{9,8},{10,11... | collective-permute-start | bytes 1769480 | tf_op jit(solution)/shard_map/ppermute | solution.py:483
  81.5 4.6 %collective-permute-start.21 = (f32[24,128]{1,0:T(8,128)S(1)}, f32[24,128]{1,0:T(8,128)S(1)}, u32[]{:S(2)}, u32[]{:S(2)}) collective-permute-start(f32[24,128]{1,0:T(8,128)S(1)} %get-tuple-element.28.r_0_), channel_id=1, source_target_pairs={{0,6},{2,0},{4,2},{6,4},{1,7},{3,1},{5,3},{7,5},{8,14},{10,8},{12,... | collective-permute-start | bytes 36872 | tf_op jit(solution)/shard_map/ppermute | solution.py:483
  84.7 5.2 %collective-permute-start.20 = (f32[24,128]{1,0:T(8,128)S(1)}, f32[24,128]{1,0:T(8,128)S(1)}, u32[]{:S(2)}, u32[]{:S(2)}) collective-permute-start(f32[24,128]{1,0:T(8,128)S(1)} %get-tuple-element.28.r_0_), channel_id=1, source_target_pairs={{0,4},{2,6},{4,0},{6,2},{1,5},{3,7},{5,1},{7,3},{8,12},{10,14},{12... | collective-permute-start | bytes 36872 | tf_op jit(solution)/shard_map/ppermute | solution.py:483
  84.8 5.2 %collective-permute-start.19 = (f32[24,128]{1,0:T(8,128)S(1)}, f32[24,128]{1,0:T(8,128)S(1)}, u32[]{:S(2)}, u32[]{:S(2)}) collective-permute-start(f32[24,128]{1,0:T(8,128)S(1)} %get-tuple-element.28.r_0_), channel_id=1, source_target_pairs={{0,2},{2,4},{4,6},{6,0},{1,3},{3,5},{5,7},{7,1},{8,10},{10,12},{12... | collective-permute-start | bytes 36872 | tf_op jit(solution)/shard_map/ppermute | solution.py:483
  86.1 9.4 %collective-permute-start.25 = (bf16[192,768]{1,0:T(8,128)(2,1)S(1)}, bf16[192,768]{1,0:T(8,128)(2,1)S(1)}, u32[]{:S(2)}, u32[]{:S(2)}) collective-permute-start(bf16[192,768]{1,0:T(8,128)(2,1)S(1)} %slice.40), channel_id=1, source_target_pairs={{0,8},{8,16},{16,24},{24,0},{1,9},{9,17},{17,25},{25,1},{2,10},{10... | collective-permute-start | bytes 884744 | tf_op jit(solution)/shard_map/ppermute | solution.py:483
  89.9 5.6 %collective-permute-start.35 = (bf16[192,768]{1,0:T(8,128)(2,1)S(1)}, bf16[192,768]{1,0:T(8,128)(2,1)S(1)}, u32[]{:S(2)}, u32[]{:S(2)}) collective-permute-start(bf16[192,768]{1,0:T(8,128)(2,1)S(1)} %collective-permute-done.30.refs_7_), channel_id=1, source_target_pairs={{0,1},{1,0},{2,3},{3,2},{4,5},{5,4},{6,7},{7,6},{8,9},{9,8},{10,11... | collective-permute-start | bytes 884744 | tf_op jit(solution)/shard_map/ppermute | solution.py:483
  90.0 5.6 %collective-permute-start.34 = (bf16[192,768]{1,0:T(8,128)(2,1)S(1)}, bf16[192,768]{1,0:T(8,128)(2,1)S(1)}, u32[]{:S(2)}, u32[]{:S(2)}) collective-permute-start(bf16[192,768]{1,0:T(8,128)(2,1)S(1)} %collective-permute-done.29.refs_6_), channel_id=1, source_target_pairs={{0,1},{1,0},{2,3},{3,2},{4,5},{5,4},{6,7},{7,6},{8,9},{9,8},{10,11... | collective-permute-start | bytes 884744 | tf_op jit(solution)/shard_map/ppermute | solution.py:483
  95.5 19.6 %collective-permute-start.22 = (f32[24,128]{1,0:T(8,128)S(1)}, f32[24,128]{1,0:T(8,128)S(1)}, u32[]{:S(2)}, u32[]{:S(2)}) collective-permute-start(f32[24,128]{1,0:T(8,128)S(1)} %fold_y1.1.mine), channel_id=1, source_target_pairs={{0,1},{1,0},{2,3},{3,2},{4,5},{5,4},{6,7},{7,6},{8,9},{9,8},{10,11... | collective-permute-start | bytes 36872 | tf_op jit(solution)/shard_map/ppermute | solution.py:483
  117.6 3.8 %collective-permute-start.38 = (f32[32,128]{1,0:T(8,128)S(1)}, f32[32,128]{1,0:T(8,128)S(1)}, u32[]{:S(2)}, u32[]{:S(2)}) collective-permute-start(f32[32,128]{1,0:T(8,128)S(1)} %get-tuple-element.31.p0), channel_id=1, source_target_pairs={{0,24},{8,0},{16,8},{24,16},{1,25},{9,1},{17,9},{25,17},{2,26},{10... | collective-permute-start | bytes 49160 | tf_op jit(solution)/shard_map/ppermute | solution.py:483
  117.7 5.3 %collective-permute-start.37 = (f32[32,128]{1,0:T(8,128)S(1)}, f32[32,128]{1,0:T(8,128)S(1)}, u32[]{:S(2)}, u32[]{:S(2)}) collective-permute-start(f32[32,128]{1,0:T(8,128)S(1)} %get-tuple-element.31.p0), channel_id=1, source_target_pairs={{0,16},{8,24},{16,0},{24,8},{1,17},{9,25},{17,1},{25,9},{2,18},{10... | collective-permute-start | bytes 49160 | tf_op jit(solution)/shard_map/ppermute | solution.py:483
  120.0 4.9 %collective-permute-start.36 = (f32[32,128]{1,0:T(8,128)S(1)}, f32[32,128]{1,0:T(8,128)S(1)}, u32[]{:S(2)}, u32[]{:S(2)}) collective-permute-start(f32[32,128]{1,0:T(8,128)S(1)} %get-tuple-element.31.p0), channel_id=1, source_target_pairs={{0,8},{8,16},{16,24},{24,0},{1,9},{9,17},{17,25},{25,1},{2,10},{10... | collective-permute-start | bytes 49160 | tf_op jit(solution)/shard_map/ppermute | solution.py:483
  138.1 4.8 %collective-permute-start.41 = (f32[40,128]{1,0:T(8,128)S(1)}, f32[40,128]{1,0:T(8,128)S(1)}, u32[]{:S(2)}, u32[]{:S(2)}) collective-permute-start(f32[40,128]{1,0:T(8,128)S(1)} %get-tuple-element.33.r_0_), channel_id=1, source_target_pairs={{0,6},{2,0},{4,2},{6,4},{1,7},{3,1},{5,3},{7,5},{8,14},{10,8},{12,... | collective-permute-start | bytes 61448 | tf_op jit(solution)/shard_map/ppermute | solution.py:483
  141.4 5.3 %collective-permute-start.40 = (f32[40,128]{1,0:T(8,128)S(1)}, f32[40,128]{1,0:T(8,128)S(1)}, u32[]{:S(2)}, u32[]{:S(2)}) collective-permute-start(f32[40,128]{1,0:T(8,128)S(1)} %get-tuple-element.33.r_0_), channel_id=1, source_target_pairs={{0,4},{2,6},{4,0},{6,2},{1,5},{3,7},{5,1},{7,3},{8,12},{10,14},{12... | collective-permute-start | bytes 61448 | tf_op jit(solution)/shard_map/ppermute | solution.py:483
  142.4 5.0 %collective-permute-start.39 = (f32[40,128]{1,0:T(8,128)S(1)}, f32[40,128]{1,0:T(8,128)S(1)}, u32[]{:S(2)}, u32[]{:S(2)}) collective-permute-start(f32[40,128]{1,0:T(8,128)S(1)} %get-tuple-element.33.r_0_), channel_id=1, source_target_pairs={{0,2},{2,4},{4,6},{6,0},{1,3},{3,5},{5,7},{7,1},{8,10},{10,12},{12... | collective-permute-start | bytes 61448 | tf_op jit(solution)/shard_map/ppermute | solution.py:483
  161.8 5.3 %collective-permute-start.44 = (f32[24,128]{1,0:T(8,128)S(1)}, f32[24,128]{1,0:T(8,128)S(1)}, u32[]{:S(2)}, u32[]{:S(2)}) collective-permute-start(f32[24,128]{1,0:T(8,128)S(1)} %step4.1.p0), channel_id=1, source_target_pairs={{0,16},{8,24},{16,0},{24,8},{1,17},{9,25},{17,1},{25,9},{2,18},{10... | collective-permute-start | bytes 36872 | tf_op jit(solution)/shard_map/ppermute | solution.py:483
  162.7 4.9 %collective-permute-start.43 = (f32[24,128]{1,0:T(8,128)S(1)}, f32[24,128]{1,0:T(8,128)S(1)}, u32[]{:S(2)}, u32[]{:S(2)}) collective-permute-start(f32[24,128]{1,0:T(8,128)S(1)} %step4.1.p0), channel_id=1, source_target_pairs={{0,8},{8,16},{16,24},{24,0},{1,9},{9,17},{17,25},{25,1},{2,10},{10... | collective-permute-start | bytes 36872 | tf_op jit(solution)/shard_map/ppermute | solution.py:483
  178.9 5.3 %collective-permute-start.47 = (f32[24,128]{1,0:T(8,128)S(1)}, f32[24,128]{1,0:T(8,128)S(1)}, u32[]{:S(2)}, u32[]{:S(2)}) collective-permute-start(f32[24,128]{1,0:T(8,128)S(1)} %get-tuple-element.37.r_0_), channel_id=1, source_target_pairs={{0,4},{2,6},{4,0},{6,2},{1,5},{3,7},{5,1},{7,3},{8,12},{10,14},{12... | collective-permute-start | bytes 36872 | tf_op jit(solution)/shard_map/ppermute | solution.py:483
  180.2 5.0 %collective-permute-start.46 = (f32[24,128]{1,0:T(8,128)S(1)}, f32[24,128]{1,0:T(8,128)S(1)}, u32[]{:S(2)}, u32[]{:S(2)}) collective-permute-start(f32[24,128]{1,0:T(8,128)S(1)} %get-tuple-element.37.r_0_), channel_id=1, source_target_pairs={{0,2},{2,4},{4,6},{6,0},{1,3},{3,5},{5,7},{7,1},{8,10},{10,12},{12... | collective-permute-start | bytes 36872 | tf_op jit(solution)/shard_map/ppermute | solution.py:483
  194.3 5.2 %collective-permute-start.51 = (f32[16,128]{1,0:T(8,128)S(1)}, f32[16,128]{1,0:T(8,128)S(1)}, u32[]{:S(2)}, u32[]{:S(2)}) collective-permute-start(f32[16,128]{1,0:T(8,128)S(1)} %get-tuple-element.38.p0), channel_id=1, source_target_pairs={{0,16},{8,24},{16,0},{24,8},{1,17},{9,25},{17,1},{25,9},{2,18},{10... | collective-permute-start | bytes 24584 | tf_op jit(solution)/shard_map/ppermute | solution.py:483
  195.2 4.9 %collective-permute-start.50 = (f32[16,128]{1,0:T(8,128)S(1)}, f32[16,128]{1,0:T(8,128)S(1)}, u32[]{:S(2)}, u32[]{:S(2)}) collective-permute-start(f32[16,128]{1,0:T(8,128)S(1)} %get-tuple-element.38.p0), channel_id=1, source_target_pairs={{0,8},{8,16},{16,24},{24,0},{1,9},{9,17},{17,25},{25,1},{2,10},{10... | collective-permute-start | bytes 24584 | tf_op jit(solution)/shard_map/ppermute | solution.py:483
  (20 other events, 311.0 us)
